TPU v7x, 128 devices: a whole 4x4x4 slice. The times are simulated.
128 devices in a mesh: dp: 16 (over y, z), mp: 8 (over x, core).
Axes of the slice: x: 4, y: 4, z: 4, core: 2. Of those that a mesh axis runs over, the one named last changes fastest.
Arguments:
- enc: bfloat16 [4096, 4096], P(('dp', 'mp')), may hold values from -76 to 76
- enc_owner: int32 [4096], P(('dp', 'mp')), may hold values from 0 to 15, as said below
- enc_example: int32 [4096], P(('dp', 'mp')), may hold values from 0 to 7, as said below
- dec: bfloat16 [4096, 4096], P('dp'), may hold values from -36 to 36
- dec_lengths: int32 [16, 8], P('dp'), may hold values from 1 to 64, 256 in all within a row
- norm_gain: bfloat16 [4096], replicated, may hold values from 0.25 to 1.75
- w_query: bfloat16 [4096, 4096], P(None, 'mp'), may hold values from -0.0625 to 0.0625
- w_key: bfloat16 [4096, 4096], P(None, 'mp'), may hold values from -0.0625 to 0.0625
- w_value: bfloat16 [4096, 4096], P(None, 'mp'), may hold values from -0.09375 to 0.09375
- w_out: bfloat16 [4096, 4096], P('mp'), may hold values from -0.09375 to 0.09375
- grad_out: bfloat16 [4096, 4096], P('dp'), may hold values from -12 to 12
Outputs:
- grad_dec: bfloat16 [4096, 4096], P('dp', 'mp')
- grad_enc: bfloat16 [4096, 4096], P(('dp', 'mp'))
- grad_wk: float32 [4096, 4096], P('dp', 'mp')
- grad_wv: float32 [4096, 4096], P('dp', 'mp')
Inputs may be any that keep to these rules, and one draw needn't show every extreme that they name: `enc_owner`: each device's 32 encoder rows send at most 4 rows to any one owner and at least one row to every owner; one owner, drawn from the seed, takes exactly 4 rows from every device. `enc_example`: every example of every owner has at least one encoder row. `dec_lengths`: row o holds the lengths of owner o's packed examples in order.
All inputs are finite; a program needn't handle non-finite values.
Results may differ from a plain program's by a relative error of at most 0.025.
The roundings to bfloat16 on the way count: a program that leaves them out, or rounds other values in their place, can miss the bound.
Values may be sent and summed in bfloat16 or wider, within the bound.
A program may use at most 128 MiB of HBM per device.

v0:
```python
import jax
import jax.numpy as jnp
from jax import lax
from jax.sharding import PartitionSpec as P

DH = 256


def pack_rows(enc, enc_owner, enc_example, dp_size, capacity):
    owner_ids = jnp.arange(dp_size, dtype=jnp.int32)
    onehot = (enc_owner[:, None] == owner_ids[None, :]).astype(jnp.int32)
    rank = jnp.sum((jnp.cumsum(onehot, axis=0) - onehot) * onehot, axis=1)
    target = enc_owner * capacity + rank
    placed = target[:, None] == jnp.arange(dp_size * capacity, dtype=jnp.int32)[None, :]
    placing = placed.astype(jnp.bfloat16)
    packed = lax.dot_general(
        placing, enc, (((0,), (0,)), ((), ())), preferred_element_type=jnp.float32
    ).astype(jnp.bfloat16)
    packed_example = jnp.sum(placed.astype(jnp.int32) * (enc_example + 1)[:, None], axis=0) - 1
    return (placing, packed, packed_example)


def attention_grads(query_rows, grad_rows, key_rows, value_rows, segment, slot_example):
    tgt_rows = query_rows.shape[0]
    slot_count = key_rows.shape[0]
    head_count = query_rows.shape[1] // DH
    score_scale = DH ** (-0.5)
    query_heads = query_rows.reshape(tgt_rows, head_count, DH)
    grad_heads = grad_rows.reshape(tgt_rows, head_count, DH)
    key_heads = key_rows.reshape(slot_count, head_count, DH)
    value_heads = value_rows.reshape(slot_count, head_count, DH)
    scores = (
        jnp.einsum("thd,shd->hts", query_heads, key_heads, preferred_element_type=jnp.float32)
        * score_scale
    )
    allowed = (segment[:, None] == slot_example[None, :])[None, :, :]
    scores = jnp.where(allowed, scores, -1e30)
    row_max = jnp.max(scores, axis=-1, keepdims=True)
    raw_weights = jnp.where(allowed, jnp.exp(scores - row_max), 0.0)
    probs_wide = raw_weights / jnp.sum(raw_weights, axis=-1, keepdims=True)
    probs_narrow = probs_wide.astype(jnp.bfloat16)
    grad_probs = jnp.einsum(
        "thd,shd->hts", grad_heads, value_heads, preferred_element_type=jnp.float32
    )
    inner_sum = jnp.sum(probs_wide * grad_probs, axis=-1, keepdims=True)
    grad_scores = (probs_wide * (grad_probs - inner_sum) * score_scale).astype(jnp.bfloat16)
    grad_query = jnp.einsum(
        "hts,shd->thd", grad_scores, key_heads, preferred_element_type=jnp.float32
    ).astype(jnp.bfloat16)
    grad_key = jnp.einsum(
        "hts,thd->shd", grad_scores, query_heads, preferred_element_type=jnp.float32
    ).astype(jnp.bfloat16)
    grad_value = jnp.einsum(
        "hts,thd->shd", probs_narrow, grad_heads, preferred_element_type=jnp.float32
    ).astype(jnp.bfloat16)
    return (
        grad_query.reshape(tgt_rows, -1),
        grad_key.reshape(slot_count, -1),
        grad_value.reshape(slot_count, -1),
    )


def local(
    enc,
    enc_owner,
    enc_example,
    dec,
    dec_lengths,
    norm_gain,
    w_query,
    w_key,
    w_value,
    w_out,
    grad_out,
):
    dp_size = lax.axis_size("dp")
    mp_size = lax.axis_size("mp")
    row_count = enc.shape[0]
    features = enc.shape[1]
    capacity = 2 * row_count // dp_size
    placing, packed, packed_example = pack_rows(enc, enc_owner, enc_example, dp_size, capacity)
    at_owner, owner_example = (
        lax.all_to_all(packed, "dp", split_axis=0, concat_axis=0, tiled=True),
        lax.all_to_all(packed_example, "dp", split_axis=0, concat_axis=0, tiled=True),
    )
    slot_rows, slot_example = (
        lax.all_gather(at_owner, "mp", axis=0, tiled=True),
        lax.all_gather(owner_example, "mp", axis=0, tiled=True),
    )
    dec_wide = dec.astype(jnp.float32)
    root_mean = jnp.sqrt(jnp.mean(dec_wide * dec_wide, axis=-1, keepdims=True) + 1e-06)
    unit_rows = dec_wide / root_mean
    gain_wide = norm_gain.astype(jnp.float32)
    normed = (unit_rows * gain_wide[None, :]).astype(jnp.bfloat16)
    query_rows = jnp.dot(normed, w_query, preferred_element_type=jnp.float32).astype(jnp.bfloat16)
    key_rows = jnp.dot(slot_rows, w_key, preferred_element_type=jnp.float32).astype(jnp.bfloat16)
    value_rows = jnp.dot(slot_rows, w_value, preferred_element_type=jnp.float32).astype(
        jnp.bfloat16
    )
    grad_context = lax.dot_general(
        grad_out, w_out, (((1,), (1,)), ((), ())), preferred_element_type=jnp.float32
    ).astype(jnp.bfloat16)
    places = jnp.arange(dec.shape[0], dtype=jnp.int32)
    bounds = jnp.cumsum(dec_lengths[0])
    segment = jnp.sum((bounds[None, :] <= places[:, None]).astype(jnp.int32), axis=1)
    grad_query, grad_key, grad_value = attention_grads(
        query_rows, grad_context, key_rows, value_rows, segment, slot_example
    )
    term = lax.dot_general(
        grad_key, w_key, (((1,), (1,)), ((), ())), preferred_element_type=jnp.float32
    )
    summed = lax.psum_scatter(
        (
            term
            + lax.dot_general(
                grad_value, w_value, (((1,), (1,)), ((), ())), preferred_element_type=jnp.float32
            )
        ).astype(jnp.bfloat16),
        "mp",
        scatter_dimension=0,
        tiled=True,
    )
    back_rows = lax.all_to_all(summed, "dp", split_axis=0, concat_axis=0, tiled=True)
    grad_enc = jnp.dot(placing, back_rows, preferred_element_type=jnp.float32).astype(jnp.bfloat16)
    both_grads = jnp.concatenate([grad_key, grad_value], axis=1)
    weight_share = lax.psum_scatter(
        lax.dot_general(
            slot_rows, both_grads, (((0,), (0,)), ((), ())), preferred_element_type=jnp.float32
        ).astype(jnp.bfloat16),
        "dp",
        scatter_dimension=0,
        tiled=True,
    ).astype(jnp.float32)
    local_width = w_key.shape[1]
    grad_wk = weight_share[:, :local_width]
    grad_wv = weight_share[:, local_width:]
    query_term = lax.dot_general(
        grad_query, w_query, (((1,), (1,)), ((), ())), preferred_element_type=jnp.float32
    )
    share_width = features // mp_size
    share_start = lax.axis_index("mp") * share_width
    whole_sum = lax.psum(query_term.astype(jnp.bfloat16), "mp").astype(jnp.float32)
    scaled = whole_sum * gain_wide[None, :]
    inner_mean = jnp.mean(scaled * unit_rows, axis=-1, keepdims=True)
    result = (scaled - unit_rows * inner_mean) / root_mean
    grad_dec = lax.dynamic_slice_in_dim(result, share_start, share_width, 1).astype(jnp.bfloat16)
    return (grad_dec, grad_enc, grad_wk, grad_wv)


def solution(mesh):
    placed = (
        P(("dp", "mp"), None),
        P(("dp", "mp")),
        P(("dp", "mp")),
        P("dp", None),
        P("dp", None),
        P(),
        P(None, "mp"),
        P(None, "mp"),
        P(None, "mp"),
        P("mp", None),
        P("dp", None),
    )
    return jax.shard_map(
        local,
        mesh=mesh,
        in_specs=placed,
        out_specs=(P("dp", "mp"), P(("dp", "mp"), None), P("dp", "mp"), P("dp", "mp")),
        check_vma=False,
    )
```

profile of v0, /device:TPU:1, one launch (start us, length us, event | category | flops | bytes accessed | tf_op | source)
XLA Modules:
  0.0 289.2 jit_solution(3050890514533664740)
XLA Ops:
  7.2 0.9 fusion.26
  8.2 0.8 select_reduce_fusion.1
  9.0 0.7 multiply_add_fusion
  9.7 1.4 convolution_convert_fusion.2
  11.3 18.7 %all_to_all.33 = bf16[16,4,4096]{2,1,0:T(4,128)(2,1)S(1)} all-to-all(bf16[16,4,4096]{2,1,0:T(4,128)(2,1)S(1)} %all_to_all.22), channel_id=1, replica_groups=mesh['dp'=16,'mp'=8] {'dp'}, dimensions={0} | all-to-all | bytes 1048576 | tf_op jit(solution)/shard_map/all_to_all | solution.py:83
  30.0 0.9 all_to_all.24
  31.0 0.7 sub.30
  31.7 3.5 %all-to-all-start.1 = ((s32[16,4,1]{1,2,0:T(1,128)}), s32[16,4,1]{1,2,0:T(1,128)S(1)}, u32[]{:S(2)}, u32[]{:S(2)}) async-start(s32[16,4,1]{1,2,0:T(1,128)} %bitcast.3), calls=%async_computation.1 | async-start | bytes 16384 | tf_op jit(solution)/shard_map/all_to_all | solution.py:84
  35.4 2.1 fusion.2
  37.5 4.4 %fusion.13 = bf16[256,512]{1,0:T(8,128)(2,1)S(1)} fusion(bf16[4096,512]{1,0:T(8,128)(2,1)} %param.17, f32[4096]{0:T(1024)S(1)} %convert_element_type.82, bf16[256,4096]{1,0:T(8,128)(2,1)} %param.14, f32[256]{0:T(256)S(1)} %add_sqrt_fusion), kind=kOutput, calls=%fused_computation.28 | convolution fusion | flops 1078067200 | bytes 6571008 | tf_op jit(solution)/shard_map/dot_general | solution.py:95
  42.1 3.5 %convolution_convert_fusion.8 = bf16[256,512]{1,0:T(8,128)(2,1)S(1)} fusion(bf16[256,4096]{1,0:T(8,128)(2,1)S(1)} %copy-done, bf16[512,4096]{1,0:T(8,128)(2,1)} %param.20), kind=kOutput, calls=%fused_computation.29 | convolution fusion | flops 1073872896 | bytes 6553600 | tf_op jit(solution)/shard_map/dot_general | solution.py:100
  48.6 10.1 %all-reduce = s32[512]{0:T(512)S(1)} all-reduce(s32[512]{0:T(512)S(1)} %dynamic-update-slice), channel_id=1, replica_groups=mesh['dp'=16,'mp'=8] {'mp'}, use_global_device_ids=true, to_apply=%add | all-reduce | flops 512 | bytes 4096
  58.8 4.1 %all-gather.2.cloned.1.call-done = bf16[512,4096]{1,0:T(8,128)(2,1)} async-done(((bf16[64,4096]{1,0:T(8,128)(2,1)}), bf16[512,4096]{1,0:T(8,128)(2,1)}) %all-gather.2.cloned.1.call-update) | async-done | bytes 4194320 | tf_op jit(solution)/shard_map/all_gather | solution.py:87
  62.9 6.0 %convolution_convert_fusion.6 = bf16[512,512]{0,1:T(8,128)(2,1)S(1)} fusion(bf16[512,4096]{1,0:T(8,128)(2,1)} %all-gather.2.cloned.1.call-done, bf16[4096,512]{1,0:T(8,128)(2,1)} %param.19), kind=kOutput, calls=%fused_computation.25 | convolution fusion | flops 2147745792 | bytes 8912896 | tf_op jit(solution)/shard_map/dot_general | solution.py:97
  69.3 2.4 convolution_convert_fusion.7
  71.7 1.6 fusion.38
  73.3 1.9 convolution_convert_fusion.4
  75.2 4.1 %convolution_convert_fusion.5 = bf16[2,256,512]{2,1,0:T(8,128)(2,1)S(1)} fusion(bf16[256,2,256]{0,2,1:T(8,128)(2,1)S(1)} %bitcast.53, f32[2,256,512]{2,1,0:T(8,128)S(1)} %fusion.39, f32[2,256,512]{2,1,0:T(8,128)} %get-tuple-element.10, f32[2,256]{1,0:T(2,128)S(1)} %get-tuple-element.9), kind=kOutput, calls=%fused_computation.24 | convolution fusion | flops 136315904 | bytes 2885632 | tf_op jit(solution)/shard_map/hts,thd->shd/dot_general | solution.py:50
  79.4 4.7 %fusion.40 = f32[512,4096]{1,0:T(8,128)S(1)} fusion(bf16[512,512]{0,1:T(8,128)(2,1)S(1)} %bitcast.47, bf16[4096,512]{1,0:T(8,128)(2,1)} %param.18), kind=kOutput, calls=%fused_computation.71 | convolution fusion | flops 2147483648 | bytes 13107200 | tf_op jit(solution)/shard_map/dot_general | solution.py:109
  84.1 4.7 %add_convert_fusion = bf16[512,4096]{1,0:T(8,128)(2,1)} fusion(f32[512,4096]{1,0:T(8,128)S(1)} %fusion.40, bf16[512,512]{0,1:T(8,128)(2,1)S(1)} %bitcast.43, bf16[4096,512]{1,0:T(8,128)(2,1)S(1)} %copy-done.3), kind=kOutput, calls=%fused_computation.2 | convolution fusion | flops 2151677952 | bytes 17301504 | tf_op jit(solution)/shard_map/dot_general | solution.py:115
  88.9 4.0 %convolution_convert_fusion.9 = bf16[2,256,256]{2,1,0:T(8,128)(2,1)S(1)} fusion(bf16[512,2,256]{0,2,1:T(8,128)(2,1)} %bitcast.57, f32[2,256,512]{2,1,0:T(8,128)S(1)} %fusion.39, f32[2,256,512]{2,1,0:T(8,128)} %get-tuple-element.10, f32[2,256]{1,0:T(2,128)S(1)} %get-tuple-element.9), kind=kOutput, calls=%fused_computation.30 | convolution fusion | flops 136184832 | bytes 2885632 | tf_op jit(solution)/shard_map/hts,shd->thd/dot_general | solution.py:47
  92.9 4.8 %convolution_convert_fusion.1 = bf16[256,4096]{1,0:T(8,128)(2,1)} fusion(bf16[256,512]{0,1:T(8,128)(2,1)S(1)} %bitcast.50, bf16[4096,512]{1,0:T(8,128)(2,1)} %param.17), kind=kOutput, calls=%fused_computation.6 | convolution fusion | flops 1074790400 | bytes 6553600 | tf_op jit(solution)/shard_map/dot_general | solution.py:137
  97.8 10.0 %convolution_convert_fusion = bf16[4096,1024]{1,0:T(8,128)(2,1)} fusion(bf16[512,4096]{1,0:T(8,128)(2,1)} %all-gather.2.cloned.1.call-done, bf16[512,512]{0,1:T(8,128)(2,1)S(1)} %bitcast.44, bf16[512,512]{0,1:T(8,128)(2,1)S(1)} %bitcast.48), kind=kOutput, calls=%fused_computation.3 | convolution fusion | flops 4301258752 | bytes 13631488 | tf_op jit(solution)/shard_map/dot_general | solution.py:127
  107.8 15.7 %reduce-scatter.3.cloned.1.call-done = bf16[64,4096]{1,0:T(8,128)(2,1)} async-done(((bf16[512,4096]{1,0:T(8,128)(2,1)}), bf16[64,4096]{1,0:T(8,128)(2,1)}) %reduce-scatter.3.cloned.1.call-update) | async-done | bytes 524304 | tf_op jit(solution)/shard_map/reduce_scatter | solution.py:112
  123.5 2.0 all_to_all.27
  125.5 6.8 %all-to-all-start.2 = ((bf16[16,4,4096]{2,1,0:T(4,128)(2,1)}), bf16[16,4,4096]{2,1,0:T(4,128)(2,1)S(1)}, u32[]{:S(2)}, u32[]{:S(2)}) async-start(bf16[16,4,4096]{2,1,0:T(4,128)(2,1)} %all_to_all.27), calls=%async_computation.3 | async-start | bytes 1048576 | tf_op jit(solution)/shard_map/all_to_all | solution.py:123
  132.3 59.3 %all-reduce.3.cloned.1.call-done = bf16[256,4096]{1,0:T(8,128)(2,1)} async-done(((bf16[256,4096]{1,0:T(8,128)(2,1)}), bf16[256,4096]{1,0:T(8,128)(2,1)}) %all-reduce.3.cloned.1.call-update) | async-done | bytes 2097168 | tf_op jit(solution)/shard_map/psum | solution.py:142
  191.6 3.3 %multiply_reduce_fusion = (f32[256]{0:T(256)S(1)}, f32[256,4096]{1,0:T(8,128)S(1)}, f32[256,4096]{1,0:T(8,128)S(1)}) fusion(f32[4096]{0:T(1024)S(1)} %convert_element_type.82, bf16[256,4096]{1,0:T(8,128)(2,1)} %all-reduce.3.cloned.1.call-done, f32[256]{0:T(256)S(1)} %add_sqrt_fusion, bf16[256,4096]{1,0:T(8,128)(2,1)} %param.14), kind=kLoop, calls=%fused_computation.10 | loop fusion | flops 6291200 | bytes 12601344 | tf_op jit(solution)/shard_map/reduce_sum | solution.py:144
  194.9 0.9 fusion.22
  195.9 1.0 convolution_convert_fusion.3
  196.9 83.6 %reduce-scatter.5.cloned.1.call-done = bf16[256,1024]{1,0:T(8,128)(2,1)} async-done(((bf16[4096,1024]{1,0:T(8,128)(2,1)}), bf16[256,1024]{1,0:T(8,128)(2,1)}) %reduce-scatter.5.cloned.1.call-update) | async-done | bytes 524304 | tf_op jit(solution)/shard_map/reduce_scatter | solution.py:126
  280.5 2.1 fusion.37
  (48 shorter events, 3.9 us)
Async XLA Ops:
  7.2 34.9 %copy-start = (bf16[256,4096]{1,0:T(8,128)(2,1)S(1)}, bf16[256,4096]{1,0:T(8,128)(2,1)}, u32[]{:S(2)}) copy-start(bf16[256,4096]{1,0:T(8,128)(2,1)} %param.21) | copy-start | bytes 6291460
  7.2 28.1 %copy-start.6 = (s32[1,8]{1,0:T(1,128)S(1)}, s32[1,8]{1,0:T(1,128)}, u32[]{:S(2)}) copy-start(s32[1,8]{1,0:T(1,128)} %param.15) | copy-start | bytes 100
  7.2 28.2 %copy-start.4 = (bf16[4096]{0:T(1024)(128)(2,1)S(1)}, bf16[4096]{0:T(1024)(128)(2,1)}, u32[]{:S(2)}) copy-start(bf16[4096]{0:T(1024)(128)(2,1)} %param.16) | copy-start | bytes 24580
  7.2 55.7 %all-gather.2.cloned.1.call-start = ((), (), s32[]{:S(2)}) async-start(), calls=%async_computation.5 | async-start | bytes 4718592 | tf_op jit(solution)/shard_map/all_gather | solution.py:87
  31.7 15.4 %all-to-all-start.1 = ((s32[16,4,1]{1,2,0:T(1,128)}), s32[16,4,1]{1,2,0:T(1,128)S(1)}, u32[]{:S(2)}, u32[]{:S(2)}) async-start(s32[16,4,1]{1,2,0:T(1,128)} %bitcast.3), calls=%async_computation.1 | async-start | bytes 16384 | tf_op jit(solution)/shard_map/all_to_all | solution.py:84
  35.2 88.3 %reduce-scatter.3.cloned.1.call-start = ((), (), s32[]{:S(2)}) async-start(), calls=%async_computation.7 | async-start | bytes 4718592 | tf_op jit(solution)/shard_map/reduce_scatter | solution.py:112
  42.1 3.7 %copy-start.8 = (u32[128]{0:T(128)S(1)}, u32[128]{0:T(128)}, u32[]{:S(2)}) copy-start(u32[128]{0:T(128)} %constant.45) | copy-start | bytes 1540
  62.9 6.3 %copy-start.2 = (bf16[4096,512]{1,0:T(8,128)(2,1)S(1)}, bf16[4096,512]{1,0:T(8,128)(2,1)}, u32[]{:S(2)}) copy-start(bf16[4096,512]{1,0:T(8,128)(2,1)} %param.18) | copy-start | bytes 12582916
  62.9 6.3 %copy-start.5 = (bf16[512,4096]{1,0:T(8,128)(2,1)S(1)}, bf16[512,4096]{1,0:T(8,128)(2,1)}, u32[]{:S(2)}) copy-start(bf16[512,4096]{1,0:T(8,128)(2,1)} %all-gather.2.cloned.1.call-done) | copy-start | bytes 12582916
  71.7 1.6 copy-start.7
  79.3 4.8 %copy-start.3 = (bf16[4096,512]{1,0:T(8,128)(2,1)S(1)}, bf16[4096,512]{1,0:T(8,128)(2,1)}, u32[]{:S(2)}) copy-start(bf16[4096,512]{1,0:T(8,128)(2,1)} %param.19) | copy-start | bytes 12582916
  88.8 102.8 %all-reduce.3.cloned.1.call-start = ((), (), s32[]{:S(2)}) async-start(), calls=%async_computation.6 | async-start | bytes 4194304 | tf_op jit(solution)/shard_map/psum | solution.py:142
  97.7 182.8 %reduce-scatter.5.cloned.1.call-start = ((), (), s32[]{:S(2)}) async-start(), calls=%async_computation.8 | async-start | bytes 8912896 | tf_op jit(solution)/shard_map/reduce_scatter | solution.py:126
  125.5 70.3 %all-to-all-start.2 = ((bf16[16,4,4096]{2,1,0:T(4,128)(2,1)}), bf16[16,4,4096]{2,1,0:T(4,128)(2,1)S(1)}, u32[]{:S(2)}, u32[]{:S(2)}) async-start(bf16[16,4,4096]{2,1,0:T(4,128)(2,1)} %all_to_all.27), calls=%async_computation.3 | async-start | bytes 1048576 | tf_op jit(solution)/shard_map/all_to_all | solution.py:123
  191.6 91.0 %copy-start.1 = (bf16[256,4096]{1,0:T(8,128)(2,1)S(1)}, bf16[256,4096]{1,0:T(8,128)(2,1)}, u32[]{:S(2)}) copy-start(bf16[256,4096]{1,0:T(8,128)(2,1)} %param.21) | copy-start | bytes 6291460
Sparse Core Ops, SparseCore 0:
  31.0 31.8 all-gather.1
  88.9 34.4 reduce-scatter.2
  125.9 65.7 all-reduce.2
  194.9 85.5 reduce-scatter.4
where the time goes:
time: 290 us; the launch traced here: 289 us
  waiting for transfers between devices  163 us (56%)
  matrix products  54.8 us (19%)
  blocking collectives  28.8 us (10%)
  between operations  14.7 us (5%)
  starting transfers between devices  10.5 us (4%)
  other arithmetic  9.89 us (3%)
  local copies, waits for them, and re-layouts  7.82 us (3%)
    reduce_scatter x1, waiting for transfers between devices, local(): lax.psum_scatter(lax.dot_general(slot_rows, both_grads, (((0,), (0,)), ((...  83.6 us
    psum x1, waiting for transfers between devices, local(): lax.psum(query_term.astype(jnp.bfloat16), 'mp').astype(jnp.float32)  59.3 us
    all_to_all x1, blocking collectives, local(): lax.all_to_all(packed, 'dp', split_axis=0, concat_axis=0, tiled=True)  18.7 us
    reduce_scatter x1, waiting for transfers between devices, local(): lax.psum_scatter((term + lax.dot_general(grad_value, w_value, (((1,), (1,...  15.7 us
    unnamed x1, blocking collectives  10.1 us
    dot_general x1, matrix products, local(): lax.dot_general(slot_rows, both_grads, (((0,), (0,)), ((), ())), preferre...  10 us
    all_to_all x1, starting transfers between devices, local(): lax.all_to_all(summed, 'dp', split_axis=0, concat_axis=0, tiled=True)  6.81 us
    dot_general x1, matrix products, local(): jnp.dot(slot_rows, w_value, preferred_element_type=jnp.float32)  5.97 us
  transfers between devices with their start and end apart: 6, of which 4 were waited for; matrix products, arithmetic and copies ran while one was open for 13% of the time, Pallas kernels for 0%

commit v1 on v0

v1 whole, which is shorter than its diff:
```python
import functools

import jax
import jax.numpy as jnp
from jax import lax
from jax.experimental import pallas as pl
from jax.experimental.pallas import tpu as pltpu
from jax.sharding import PartitionSpec as P

MESH = pl.DeviceIdType.MESH
BF = jnp.bfloat16
F32 = jnp.float32
DH = 256
D = 4096
NT = (((1,), (1,)), ((), ()))
TN = (((0,), (0,)), ((), ()))


def dot(a, b):
    return jnp.dot(a, b, preferred_element_type=F32)


def dot_nt(a, b):
    return lax.dot_general(a, b, NT, preferred_element_type=F32)


def dot_tn(a, b):
    return lax.dot_general(a, b, TN, preferred_element_type=F32)


def add4(value, step):
    return lax.rem(value + step, 4)


def kernel(
    enc_ref,
    info_ref,
    len_ref,
    gain_ref,
    dec_hbm,
    go_hbm,
    wq_hbm,
    wk_hbm,
    wv_hbm,
    wo_hbm,
    gd_ref,
    ge_ref,
    gwk_ref,
    gwv_ref,
    dec_v,
    go_v,
    wq_v,
    wk_v,
    wv_v,
    wo_v,
    enc_all,
    normed,
    rms_v,
    info_all,
    q_v,
    gc_v,
    gq_v,
    place_t,
    kv0_s,
    kv1_s,
    kv0_r,
    kv1_r,
    ret_s,
    ret_r,
    g_own,
    g_all,
    ep,
    ep_t,
    gw_s,
    gw_r,
    gn_t,
    gn_sib,
    gn_s,
    gn_r,
    ge_t,
    ge_sib,
    ge_s,
    ge_r,
    rd_all,
    load_sem,
    enc_ss,
    enc_rs,
    info_ss,
    info_rs,
    epz_ss,
    epz_rs,
    ep_ss,
    ep_rs,
    kv_ss,
    kv_rs,
    ret_ss,
    ret_rs,
    rd_ss,
    rd_rs,
    gn_ss,
    gn_rs,
    ge_ss,
    ge_rs,
    gz_ss,
    gz_rs,
    gy_ss,
    gy_rs,
):
    dp = lax.axis_index("dp")
    mp = lax.axis_index("mp")
    y, z = dp // 4, lax.rem(dp, 4)
    x, c = mp // 2, lax.rem(mp, 2)
    other = 1 - c
    sib = (dp, x * 2 + other)

    def at_x(step):
        return (dp, add4(x, step) * 2 + c)

    def at_y(step):
        return (add4(y, step) * 4 + z, mp)

    def at_z(step):
        return (y * 4 + add4(z, step), mp)

    dp_peers = [(lax.rem(dp + i, 16), mp) for i in range(1, 16)]
    mp_peers = [(dp, lax.rem(mp + i, 8)) for i in range(1, 8)]

    def remote(src, dst, ss, rs, who):
        return pltpu.make_async_remote_copy(
            src_ref=src, dst_ref=dst, send_sem=ss, recv_sem=rs, device_id=who, device_id_type=MESH
        )

    loads = [
        pltpu.make_async_copy(src, dst, load_sem.at[i])
        for i, (src, dst) in enumerate(
            [
                (dec_hbm, dec_v),
                (wq_hbm, wq_v),
                (go_hbm, go_v),
                (wo_hbm, wo_v),
                (wk_hbm, wk_v),
                (wv_hbm, wv_v),
            ]
        )
    ]
    for copy in loads:
        copy.start()

    lane = lax.broadcasted_iota(jnp.int32, (8, 256), 1)
    info_all[mp] = jnp.where(lax.shift_right_logical(lane, 5) == mp, info_ref[...], 0)
    enc_all[mp] = enc_ref[...]

    barrier = pltpu.get_barrier_semaphore()
    for peer in dp_peers + mp_peers:
        pl.semaphore_signal(barrier, inc=1, device_id=peer, device_id_type=MESH)
    pl.semaphore_wait(barrier, 22)

    enc_x = {
        s: remote(enc_ref, enc_all.at[mp], enc_ss.at[s], enc_rs.at[s], at_x(s)) for s in (2, 1, 3)
    }
    for s in (2, 1, 3):
        enc_x[s].start()
    info_c = [
        remote(info_all.at[mp], info_all.at[mp], info_ss.at[i], info_rs.at[i], peer)
        for i, peer in enumerate(mp_peers)
    ]
    for copy in info_c:
        copy.start()

    def enc_forward(s):
        slot = add4(x, 4 - s) * 2 + c
        return remote(enc_all.at[slot], enc_all.at[slot], enc_ss.at[4 + s], enc_rs.at[4 + s], sib)

    enc_f = {s: enc_forward(s) for s in (1, 2, 3)}
    enc_f[0] = remote(enc_ref, enc_all.at[mp], enc_ss.at[4], enc_rs.at[4], sib)
    enc_f[0].start()
    epz = []
    for s in (1, 2, 3):
        for b in range(4):
            column = pl.multiple_of((b * 4 + add4(z, s)) * 256, 256)
            epz.append(
                remote(
                    enc_ref.at[:, pl.ds(column, 256)],
                    ep.at[z, mp, :, pl.ds(b * 256, 256)],
                    epz_ss.at[(s - 1) * 4 + b],
                    epz_rs.at[(s - 1) * 4 + b],
                    at_z(s),
                )
            )
    for copy in epz:
        copy.start()
    for b in range(4):
        column = pl.multiple_of((b * 4 + z) * 256, 256)
        ep[z, mp, :, pl.ds(b * 256, 256)] = enc_ref[:, pl.ds(column, 256)]

    loads[0].wait()

    @pl.loop(0, 8)
    def _(i):
        rows = pl.ds(pl.multiple_of(i * 32, 32), 32)
        wide = dec_v[rows, :].astype(F32)
        rms = jnp.sqrt(jnp.mean(wide * wide, axis=-1, keepdims=True) + 1e-06)
        rms_v[rows, :] = jnp.broadcast_to(rms, (32, 128))
        normed[rows, :] = ((wide / rms) * gain_ref[...].astype(F32)).astype(BF)

    loads[1].wait()
    for h in range(2):
        q_v[h] = dot(normed[...], wq_v[:, h * DH : (h + 1) * DH]).astype(BF)
    for s in (1, 3):
        enc_x[s].wait_recv()
        enc_f[s].start()
    loads[2].wait()
    loads[3].wait()
    for h in range(2):
        gc_v[h] = dot_nt(go_v[...], wo_v[h * DH : (h + 1) * DH, :]).astype(BF)

    for copy in info_c:
        copy.wait_recv()
    info = info_all[0]
    for i in range(1, 8):
        info = info + info_all[i]
    owner = info[0:1, :].astype(F32)
    example = info[1:2, :].astype(F32) + 1.0
    onehot = lax.broadcasted_iota(jnp.int32, (16, 256), 0).astype(F32) == owner
    before = lax.broadcasted_iota(jnp.int32, (256, 256), 0)
    after = lax.broadcasted_iota(jnp.int32, (256, 256), 1)
    same = lax.shift_right_logical(before, 5) == lax.shift_right_logical(after, 5)
    upper = jnp.where(same & (before < after), 1.0, 0.0).astype(BF)
    onehot = jnp.where(onehot, 1.0, 0.0)
    rank = jnp.sum(dot(onehot.astype(BF), upper) * onehot, axis=0, keepdims=True)
    block = lax.shift_right_logical(lax.broadcasted_iota(jnp.int32, (1, 256), 1), 5).astype(F32)
    target = owner * 32.0 + block * 4.0 + rank
    slot_id = lax.broadcasted_iota(jnp.int32, (512, 256), 0).astype(F32)
    placed = jnp.where(slot_id == target, 1.0, 0.0)
    place = placed.astype(BF)
    place_t[...] = placed.T.astype(BF)
    slot_example = jnp.sum(placed * example, axis=1, keepdims=True)
    kv0_s[:, :, 512:640] = jnp.broadcast_to(slot_example, (512, 128)).astype(BF).reshape(16, 32, 128)

    enc_x[2].wait_recv()
    enc_f[2].start()
    for copy in epz:
        copy.wait_recv()
    ep_x = {
        s: remote(ep.at[:, mp], ep.at[:, mp], ep_ss.at[s], ep_rs.at[s], at_x(s)) for s in (2, 1, 3)
    }
    for s in (2, 1, 3):
        ep_x[s].start()

    def ep_forward(s):
        slot = add4(x, 4 - s) * 2 + c
        return remote(ep.at[:, slot], ep.at[:, slot], ep_ss.at[4 + s], ep_rs.at[4 + s], sib)

    ep_f = {s: ep_forward(s) for s in (0, 1, 2, 3)}
    ep_f[0].start()

    for s in range(4):
        enc_f[s].wait_recv()
    loads[4].wait()
    loads[5].wait()
    kv_s, kv_r = [kv0_s, kv1_s], [kv0_r, kv1_r]
    kv_c = []
    for h in range(2):
        rows = enc_all[...].reshape(256, D)
        key = dot(rows, wk_v[:, h * DH : (h + 1) * DH]).astype(BF)
        kv_s[h][:, :, 0:256] = dot(place, key).astype(BF).reshape(16, 32, 256)
        value = dot(rows, wv_v[:, h * DH : (h + 1) * DH]).astype(BF)
        kv_s[h][:, :, 256:512] = dot(place, value).astype(BF).reshape(16, 32, 256)
        copies = [
            remote(kv_s[h].at[peer[0]], kv_r[h].at[dp], kv_ss.at[h, i], kv_rs.at[h, i], peer)
            for i, peer in enumerate(dp_peers)
        ]
        for copy in copies:
            copy.start()
        kv_r[h][dp] = kv_s[h][dp]
        kv_c.append(copies)

    place_of = lax.broadcasted_iota(jnp.int32, (1, 256), 1)
    bound = jnp.int32(0)
    segment = jnp.zeros((1, 256), jnp.int32)
    for e in range(8):
        bound = bound + len_ref[0, e]
        segment = segment + jnp.where(bound <= place_of, 1, 0)
    segment = segment.astype(F32) + 1.0

    for s in (1, 3, 2):
        ep_x[s].wait_recv()
        ep_f[s].start()

    scale = DH**-0.5
    ret_c = []
    row_dot = jnp.zeros((1, 256), F32)
    for h in range(2):
        for copy in kv_c[h]:
            copy.wait_recv()
        if h == 0:
            ex = kv0_r[:, :, 512:640].reshape(512, 128).astype(F32)
            allowed = jnp.concatenate([ex, ex], axis=1) == segment
        key = kv_r[h][:, :, 0:256].reshape(512, 256)
        value = kv_r[h][:, :, 256:512].reshape(512, 256)
        raw = dot_nt(key, q_v[h])
        scores = jnp.where(allowed, raw * scale, -1e30)
        top = jnp.max(scores, axis=0, keepdims=True)
        weights = jnp.where(allowed, jnp.exp(scores - top), 0.0)
        probs = weights / jnp.sum(weights, axis=0, keepdims=True)
        grad_probs = dot_nt(value, gc_v[h])
        inner = jnp.sum(probs * grad_probs, axis=0, keepdims=True)
        grad_scores = (probs * (grad_probs - inner) * scale).astype(BF)
        row_dot = row_dot + jnp.sum(grad_scores.astype(F32) * raw, axis=0, keepdims=True)
        ret_s[h, :, :, 0:256] = dot(grad_scores, q_v[h]).astype(BF).reshape(16, 32, 256)
        ret_s[h, :, :, 256:512] = dot(probs.astype(BF), gc_v[h]).astype(BF).reshape(16, 32, 256)
        copies = [
            remote(ret_s.at[h, peer[0]], ret_r.at[h, dp], ret_ss.at[h, i], ret_rs.at[h, i], peer)
            for i, peer in enumerate(dp_peers)
        ]
        for copy in copies:
            copy.start()
        ret_c.append(copies)
        ret_r[h, dp] = ret_s[h, dp]
        gq_v[:, h * DH : (h + 1) * DH] = dot_tn(grad_scores, key).astype(BF)

    rd_all[mp] = jnp.broadcast_to(row_dot, (8, 256))
    rd_c = [
        remote(rd_all.at[mp], rd_all.at[mp], rd_ss.at[i], rd_rs.at[i], peer)
        for i, peer in enumerate(mp_peers)
    ]
    for copy in rd_c:
        copy.start()

    gz_c = []

    def gather_z(h):
        for copy in ret_c[h]:
            copy.wait_recv()
        own = dot(place_t[...], ret_r[h].reshape(512, 512)).astype(BF)
        g_own[h] = own
        g_all[h, z] = own
        copies = [
            remote(g_own.at[h], g_all.at[h, z], gz_ss.at[h, s - 1], gz_rs.at[h, s - 1], at_z(s))
            for s in (2, 1, 3)
        ]
        for copy in copies:
            copy.start()
        gz_c.append(copies)

    gather_z(0)

    @pl.loop(0, 4)
    def _(i):
        for k in range(2):
            rows = pl.ds(pl.multiple_of((i * 2 + k) * 512, 512), 512)
            gn_t[i, k] = dot_nt(gq_v[...], wq_v[rows, :]).astype(BF)

    gn_pair = remote(gn_t.at[:, other], gn_sib, gn_ss.at[0], gn_rs.at[0], sib)
    gn_pair.start()

    gather_z(1)

    for s in range(4):
        ep_f[s].wait_recv()
    for b in range(4):
        for k in range(4):
            part = ep[k, :, :, b * 256 : (b + 1) * 256].reshape(256, 256)
            ep_t[b, :, k * 256 : (k + 1) * 256] = part.T

    gn_pair.wait_recv()

    @pl.loop(0, 4)
    def _(i):
        gn_s[i] = (gn_t[i, c].astype(F32) + gn_sib[i].astype(F32)).astype(BF)

    gn_x = [
        remote(gn_s.at[add4(x, s)], gn_r.at[s - 1], gn_ss.at[s], gn_rs.at[s], at_x(s))
        for s in (2, 1, 3)
    ]
    for copy in gn_x:
        copy.start()

    @pl.loop(0, 8)
    def _(i):
        rows = pl.ds(pl.multiple_of(i * 512, 512), 512)
        total = jnp.zeros((256, 512), F32)
        for h in range(2):
            total = total + dot_nt(g_own[h, :, 0:256], wk_v[rows, h * DH : (h + 1) * DH])
            total = total + dot_nt(g_own[h, :, 256:512], wv_v[rows, h * DH : (h + 1) * DH])
        total = total.astype(BF).reshape(4, 2, 32, 512)
        for k in range(2):
            ge_t[k, :, :, rows] = total[:, k]

    ge_pair = remote(ge_t.at[other], ge_sib, ge_ss.at[0], ge_rs.at[0], sib)
    ge_pair.start()

    gy_c = []

    def scatter_y(h):
        for copy in gz_c[h]:
            copy.wait_recv()
        every = g_all[h].reshape(1024, 512)
        copies = []
        for s in (2, 1, 3):
            gw_s[h, s - 1] = dot(ep_t[add4(y, s)], every).astype(BF)
            copy = remote(
                gw_s.at[h, s - 1], gw_r.at[h, s - 1], gy_ss.at[h, s - 1], gy_rs.at[h, s - 1], at_y(s)
            )
            copy.start()
            copies.append(copy)
        own = dot(ep_t[y], every)
        gwk_ref[:, h * DH : (h + 1) * DH] = own[:, 0:256]
        gwv_ref[:, h * DH : (h + 1) * DH] = own[:, 256:512]
        gy_c.append(copies)

    scatter_y(0)

    ge_pair.wait_recv()

    @pl.loop(0, 4)
    def _(i):
        ge_s[i] = (ge_t[c, i].astype(F32) + ge_sib[i].astype(F32)).astype(BF)

    ge_x = [
        remote(ge_s.at[add4(x, s)], ge_r.at[s - 1], ge_ss.at[s], ge_rs.at[s], at_x(s))
        for s in (2, 1, 3)
    ]
    for copy in ge_x:
        copy.start()

    scatter_y(1)

    for copy in rd_c:
        copy.wait_recv()
    inner = rd_all[0]
    for i in range(1, 8):
        inner = inner + rd_all[i]
    inner = jnp.broadcast_to(inner[0:1, :], (128, 256)).T * (1.0 / D)
    for copy in gn_x:
        copy.wait_recv()
    share = pl.ds(pl.multiple_of(mp * 512, 512), 512)
    total = gn_s[x].astype(F32)
    for s in range(3):
        total = total + gn_r[s].astype(F32)
    scaled = total * gain_ref[:, share].astype(F32)
    rms = rms_v[:, 0:1]
    unit = dec_v[:, share].astype(F32) / rms
    gd_ref[...] = ((scaled - unit * inner[:, 0:1]) / rms).astype(BF)

    for copy in ge_x:
        copy.wait_recv()
    total = ge_s[x].astype(F32)
    for s in range(3):
        total = total + ge_r[s].astype(F32)
    ge_ref[...] = total.astype(BF)

    for h in range(2):
        columns = slice(h * DH, (h + 1) * DH)
        for copy in gy_c[h]:
            copy.wait_recv()
        total = gw_r[h, 0].astype(F32) + gw_r[h, 1].astype(F32) + gw_r[h, 2].astype(F32)
        gwk_ref[:, columns] = gwk_ref[:, columns] + total[:, 0:256]
        gwv_ref[:, columns] = gwv_ref[:, columns] + total[:, 256:512]

    for copy in (
        list(enc_x.values())
        + list(enc_f.values())
        + info_c
        + epz
        + list(ep_x.values())
        + list(ep_f.values())
        + kv_c[0]
        + kv_c[1]
        + ret_c[0]
        + ret_c[1]
        + rd_c
        + gz_c[0]
        + gz_c[1]
        + [gn_pair, ge_pair]
        + gn_x
        + ge_x
        + gy_c[0]
        + gy_c[1]
    ):
        copy.wait_send()


def local(
    enc,
    enc_owner,
    enc_example,
    dec,
    dec_lengths,
    norm_gain,
    w_query,
    w_key,
    w_value,
    w_out,
    grad_out,
):
    info = jnp.tile(jnp.stack([enc_owner, enc_example]), (4, 8))
    vmem = pl.BlockSpec(memory_space=pltpu.VMEM)
    smem = pl.BlockSpec(memory_space=pltpu.SMEM)
    hbm = pl.BlockSpec(memory_space=pl.ANY)
    dma = pltpu.SemaphoreType.DMA
    V = pltpu.VMEM
    return pl.pallas_call(
        kernel,
        name="cross_attention_grads",
        out_shape=(
            jax.ShapeDtypeStruct((256, 512), BF),
            jax.ShapeDtypeStruct((32, D), BF),
            jax.ShapeDtypeStruct((256, 512), F32),
            jax.ShapeDtypeStruct((256, 512), F32),
        ),
        in_specs=[vmem, vmem, smem, vmem] + [hbm] * 6,
        out_specs=(vmem,) * 4,
        scratch_shapes=[
            V((256, D), BF),
            V((256, D), BF),
            V((D, 512), BF),
            V((D, 512), BF),
            V((D, 512), BF),
            V((512, D), BF),
            V((8, 32, D), BF),
            V((256, D), BF),
            V((256, 128), F32),
            V((8, 8, 256), jnp.int32),
            V((2, 256, 256), BF),
            V((2, 256, 256), BF),
            V((256, 512), BF),
            V((256, 512), BF),
            V((16, 32, 640), BF),
            V((16, 32, 512), BF),
            V((16, 32, 640), BF),
            V((16, 32, 512), BF),
            V((2, 16, 32, 512), BF),
            V((2, 16, 32, 512), BF),
            V((2, 256, 512), BF),
            V((2, 4, 256, 512), BF),
            V((4, 8, 32, 1024), BF),
            V((4, 256, 1024), BF),
            V((2, 3, 256, 512), BF),
            V((2, 3, 256, 512), BF),
            V((4, 2, 256, 512), BF),
            V((4, 256, 512), BF),
            V((4, 256, 512), BF),
            V((3, 256, 512), BF),
            V((2, 4, 32, D), BF),
            V((4, 32, D), BF),
            V((4, 32, D), BF),
            V((3, 32, D), BF),
            V((8, 8, 256), F32),
            dma((6,)),
            dma((8,)),
            dma((8,)),
            dma((7,)),
            dma((7,)),
            dma((12,)),
            dma((12,)),
            dma((8,)),
            dma((8,)),
            dma((2, 15)),
            dma((2, 15)),
            dma((2, 15)),
            dma((2, 15)),
            dma((7,)),
            dma((7,)),
            dma((4,)),
            dma((4,)),
            dma((4,)),
            dma((4,)),
            dma((2, 3)),
            dma((2, 3)),
            dma((2, 3)),
            dma((2, 3)),
        ],
        compiler_params=pltpu.CompilerParams(
            collective_id=0, has_side_effects=True, vmem_limit_bytes=60 * 1024 * 1024
        ),
    )(
        enc,
        info,
        dec_lengths,
        norm_gain.reshape(1, D),
        dec,
        grad_out,
        w_query,
        w_key,
        w_value,
        w_out,
    )


def solution(mesh):
    placed = (
        P(("dp", "mp"), None),
        P(("dp", "mp")),
        P(("dp", "mp")),
        P("dp", None),
        P("dp", None),
        P(),
        P(None, "mp"),
        P(None, "mp"),
        P(None, "mp"),
        P("mp", None),
        P("dp", None),
    )
    return jax.shard_map(
        local,
        mesh=mesh,
        in_specs=placed,
        out_specs=(P("dp", "mp"), P(("dp", "mp"), None), P("dp", "mp"), P("dp", "mp")),
        check_vma=False,
    )
```

time: 290 us -> 111 us (0.38)
  the two profiles are of different devices: /device:TPU:1 before, /device:TPU:96 now
where the time goes in v1:
time: 111 us
  Pallas kernels  100 us (90%)
  local copies, waits for them, and re-layouts  9.06 us (8%)
    pallas_call x1, Pallas kernels, local(): pl.pallas_call(kernel, name='cross_attention_grads', out_shape=(jax.Shape...  100 us
    unnamed x4, local copies, waits for them, and re-layouts  7.07 us

profile of v1, /device:TPU:96, one launch (start us, length us, event | category | flops | bytes accessed | tf_op | source)
XLA Modules:
  0.0 110.5 jit_solution(4324632725258429530)
XLA Ops:
  0.6 0.7 pad_add_fusion
  1.3 1.3 %reshape.12.gain_ref = bf16[1,4096]{1,0:T(2,128)(2,1)} reshape(bf16[4096]{0:T(1024)(128)(2,1)} %param.16) | data formatting | bytes 16384 | tf_op jit(solution)/shard_map/reshape | solution.py:581
  2.6 0.7 tile.10.info_ref
  3.3 100.2 %cross_attention_grads.1 = (bf16[256,512]{1,0:T(8,128)(2,1)}, bf16[32,4096]{1,0:T(8,128)(2,1)}, f32[256,512]{1,0:T(8,128)}, f32[256,512]{1,0:T(8,128)}) custom-call(bf16[32,4096]{1,0:T(8,128)(2,1)} %enc_ref.1, s32[8,256]{1,0:T(8,128)} %tile.10.info_ref, s32[1,8]{1,0:T(1,128)} %len_ref.1, bf16[1,4096]{1,0:T(2,128)(2,1)} %reshape.12.gain_ref, ...), custom_call_target="tpu_custom_call" | custom-call | tf_op jit(solution)/shard_map/cross_attention_grads/pallas_call | solution.py:503
  103.5 1.7 %copy.19 = bf16[256,512]{1,0:T(8,128)(2,1)} copy(bf16[256,512]{1,0:T(8,128)(2,1)} %get-tuple-element.8) | data formatting | bytes 524288
  105.1 1.7 %copy.20 = bf16[32,4096]{1,0:T(8,128)(2,1)} copy(bf16[32,4096]{1,0:T(8,128)(2,1)} %get-tuple-element.9) | data formatting | bytes 524288
  106.8 1.9 %copy.21 = f32[256,512]{1,0:T(8,128)} copy(f32[256,512]{1,0:T(8,128)} %get-tuple-element.10) | data formatting | bytes 1048576
  108.7 1.9 %copy.22 = f32[256,512]{1,0:T(8,128)} copy(f32[256,512]{1,0:T(8,128)} %get-tuple-element.11) | data formatting | bytes 1048576
  (1 shorter events, 0.0 us)

commit v2 on v1

--- a/solution.py
+++ b/solution.py
@@ -28,13 +28,31 @@
     return lax.dot_general(a, b, TN, preferred_element_type=F32)
 
 
+class Copy:
+    def __init__(self, copy, started):
+        self.copy, self.started, self.received = copy, started, False
+
+    def start(self):
+        self.started.append(self)
+        self.copy.start()
+
+    def wait_recv(self):
+        if not self.received:
+            self.received = True
+            self.copy.wait_recv()
+
+
+STOP = 99
+
+
 def add4(value, step):
     return lax.rem(value + step, 4)
 
 
 def kernel(
     enc_ref,
-    info_ref,
+    owner_ref,
+    example_ref,
     len_ref,
     gain_ref,
     dec_hbm,
@@ -43,6 +61,10 @@
     wk_hbm,
     wv_hbm,
     wo_hbm,
+    gd_hbm,
+    ge_hbm,
+    gwk_hbm,
+    gwv_hbm,
     gd_ref,
     ge_ref,
     gwk_ref,
@@ -83,6 +105,7 @@
     ge_r,
     rd_all,
     load_sem,
+    out_sem,
     enc_ss,
     enc_rs,
     info_ss,
@@ -125,10 +148,21 @@
     dp_peers = [(lax.rem(dp + i, 16), mp) for i in range(1, 16)]
     mp_peers = [(dp, lax.rem(mp + i, 8)) for i in range(1, 8)]
 
+    started = []
+
     def remote(src, dst, ss, rs, who):
-        return pltpu.make_async_remote_copy(
+        copy = pltpu.make_async_remote_copy(
             src_ref=src, dst_ref=dst, send_sem=ss, recv_sem=rs, device_id=who, device_id_type=MESH
         )
+        return Copy(copy, started)
+
+    def finish():
+        for i in range(1 if STOP == 0 else 6):
+            load(i)
+        for copy in started:
+            copy.wait_recv()
+        for copy in started:
+            copy.copy.wait_send()
 
     loads = [
         pltpu.make_async_copy(src, dst, load_sem.at[i])
@@ -143,11 +177,21 @@
             ]
         )
     ]
-    for copy in loads:
-        copy.start()
+    loads[0].start()
+    loaded = set()
+
+    def load(i):
+        if i not in loaded:
+            loaded.add(i)
+            loads[i].wait()
 
     lane = lax.broadcasted_iota(jnp.int32, (8, 256), 1)
-    info_all[mp] = jnp.where(lax.shift_right_logical(lane, 5) == mp, info_ref[...], 0)
+    line = lax.broadcasted_iota(jnp.int32, (8, 256), 0)
+    info = jnp.zeros((8, 256), jnp.int32)
+    for r in range(32):
+        both = jnp.where(line == 0, owner_ref[r], example_ref[r])
+        info = jnp.where(lane == mp * 32 + r, both, info)
+    info_all[mp] = info
     enc_all[mp] = enc_ref[...]
 
     barrier = pltpu.get_barrier_semaphore()
@@ -155,10 +199,12 @@
         pl.semaphore_signal(barrier, inc=1, device_id=peer, device_id_type=MESH)
     pl.semaphore_wait(barrier, 22)
 
+    if STOP == 0:
+        return finish()
     enc_x = {
         s: remote(enc_ref, enc_all.at[mp], enc_ss.at[s], enc_rs.at[s], at_x(s)) for s in (2, 1, 3)
     }
-    for s in (2, 1, 3):
+    for s in (1, 3, 2):
         enc_x[s].start()
     info_c = [
         remote(info_all.at[mp], info_all.at[mp], info_ss.at[i], info_rs.at[i], peer)
@@ -181,19 +227,35 @@
             epz.append(
                 remote(
                     enc_ref.at[:, pl.ds(column, 256)],
-                    ep.at[z, mp, :, pl.ds(b * 256, 256)],
+                    ep.at[0, z, mp, :, pl.ds(b * 256, 256)],
                     epz_ss.at[(s - 1) * 4 + b],
                     epz_rs.at[(s - 1) * 4 + b],
                     at_z(s),
                 )
             )
+        column = pl.multiple_of(add4(y, s) * 1024, 1024)
+        epz.append(
+            remote(
+                enc_ref.at[:, pl.ds(column, 1024)],
+                ep.at[1, y, mp],
+                epz_ss.at[11 + s],
+                epz_rs.at[11 + s],
+                at_y(s),
+            )
+        )
     for copy in epz:
         copy.start()
     for b in range(4):
         column = pl.multiple_of((b * 4 + z) * 256, 256)
-        ep[z, mp, :, pl.ds(b * 256, 256)] = enc_ref[:, pl.ds(column, 256)]
-
-    loads[0].wait()
+        ep[0, z, mp, :, pl.ds(b * 256, 256)] = enc_ref[:, pl.ds(column, 256)]
+    ep[1, y, mp] = enc_ref[:, pl.ds(pl.multiple_of(y * 1024, 1024), 1024)]
+
+    for copy in loads[1:]:
+        copy.start()
+
+    if STOP == 1:
+        return finish()
+    load(0)
 
     @pl.loop(0, 8)
     def _(i):
@@ -201,19 +263,23 @@
         wide = dec_v[rows, :].astype(F32)
         rms = jnp.sqrt(jnp.mean(wide * wide, axis=-1, keepdims=True) + 1e-06)
         rms_v[rows, :] = jnp.broadcast_to(rms, (32, 128))
-        normed[rows, :] = ((wide / rms) * gain_ref[...].astype(F32)).astype(BF)
-
-    loads[1].wait()
+        normed[rows, :] = ((wide / rms) * gain_ref[...].astype(F32).reshape(1, D)).astype(BF)
+
+    load(1)
     for h in range(2):
         q_v[h] = dot(normed[...], wq_v[:, h * DH : (h + 1) * DH]).astype(BF)
     for s in (1, 3):
         enc_x[s].wait_recv()
         enc_f[s].start()
-    loads[2].wait()
-    loads[3].wait()
+    if STOP == 2:
+        return finish()
+    load(2)
+    load(3)
     for h in range(2):
         gc_v[h] = dot_nt(go_v[...], wo_v[h * DH : (h + 1) * DH, :]).astype(BF)
 
+    if STOP == 3:
+        return finish()
     for copy in info_c:
         copy.wait_recv()
     info = info_all[0]
@@ -237,27 +303,31 @@
     slot_example = jnp.sum(placed * example, axis=1, keepdims=True)
     kv0_s[:, :, 512:640] = jnp.broadcast_to(slot_example, (512, 128)).astype(BF).reshape(16, 32, 128)
 
+    if STOP == 4:
+        return finish()
     enc_x[2].wait_recv()
     enc_f[2].start()
     for copy in epz:
         copy.wait_recv()
     ep_x = {
-        s: remote(ep.at[:, mp], ep.at[:, mp], ep_ss.at[s], ep_rs.at[s], at_x(s)) for s in (2, 1, 3)
+        s: remote(ep.at[:, :, mp], ep.at[:, :, mp], ep_ss.at[s], ep_rs.at[s], at_x(s)) for s in (2, 1, 3)
     }
     for s in (2, 1, 3):
         ep_x[s].start()
 
     def ep_forward(s):
         slot = add4(x, 4 - s) * 2 + c
-        return remote(ep.at[:, slot], ep.at[:, slot], ep_ss.at[4 + s], ep_rs.at[4 + s], sib)
+        return remote(ep.at[:, :, slot], ep.at[:, :, slot], ep_ss.at[4 + s], ep_rs.at[4 + s], sib)
 
     ep_f = {s: ep_forward(s) for s in (0, 1, 2, 3)}
     ep_f[0].start()
 
+    if STOP == 5:
+        return finish()
     for s in range(4):
         enc_f[s].wait_recv()
-    loads[4].wait()
-    loads[5].wait()
+    load(4)
+    load(5)
     kv_s, kv_r = [kv0_s, kv1_s], [kv0_r, kv1_r]
     kv_c = []
     for h in range(2):
@@ -275,6 +345,8 @@
         kv_r[h][dp] = kv_s[h][dp]
         kv_c.append(copies)
 
+    if STOP == 6:
+        return finish()
     place_of = lax.broadcasted_iota(jnp.int32, (1, 256), 1)
     bound = jnp.int32(0)
     segment = jnp.zeros((1, 256), jnp.int32)
@@ -283,10 +355,8 @@
         segment = segment + jnp.where(bound <= place_of, 1, 0)
     segment = segment.astype(F32) + 1.0
 
-    for s in (1, 3, 2):
-        ep_x[s].wait_recv()
-        ep_f[s].start()
-
+    if STOP == 7:
+        return finish()
     scale = DH**-0.5
     ret_c = []
     row_dot = jnp.zeros((1, 256), F32)
@@ -318,7 +388,12 @@
         ret_c.append(copies)
         ret_r[h, dp] = ret_s[h, dp]
         gq_v[:, h * DH : (h + 1) * DH] = dot_tn(grad_scores, key).astype(BF)
-
+        for s in [(1, 3), (2,)][h]:
+            ep_x[s].wait_recv()
+            ep_f[s].start()
+
+    if STOP == 8:
+        return finish()
     rd_all[mp] = jnp.broadcast_to(row_dot, (8, 256))
     rd_c = [
         remote(rd_all.at[mp], rd_all.at[mp], rd_ss.at[i], rd_rs.at[i], peer)
@@ -328,23 +403,30 @@
         copy.start()
 
     gz_c = []
-
-    def gather_z(h):
+    gather_at, reduce_at = [at_z, at_y], [at_y, at_z]
+    gather_me, reduce_me = [z, y], [y, z]
+
+    def gather(h):
+        here = gather_me[h]
         for copy in ret_c[h]:
             copy.wait_recv()
         own = dot(place_t[...], ret_r[h].reshape(512, 512)).astype(BF)
         g_own[h] = own
-        g_all[h, z] = own
+        g_all[h, here] = own
         copies = [
-            remote(g_own.at[h], g_all.at[h, z], gz_ss.at[h, s - 1], gz_rs.at[h, s - 1], at_z(s))
+            remote(
+                g_own.at[h], g_all.at[h, here], gz_ss.at[h, s - 1], gz_rs.at[h, s - 1], gather_at[h](s)
+            )
             for s in (2, 1, 3)
         ]
         for copy in copies:
             copy.start()
         gz_c.append(copies)
 
-    gather_z(0)
-
+    gather(0)
+
+    if STOP == 9:
+        return finish()
     @pl.loop(0, 4)
     def _(i):
         for k in range(2):
@@ -354,14 +436,17 @@
     gn_pair = remote(gn_t.at[:, other], gn_sib, gn_ss.at[0], gn_rs.at[0], sib)
     gn_pair.start()
 
-    gather_z(1)
-
+    gather(1)
+
+    if STOP == 10:
+        return finish()
     for s in range(4):
         ep_f[s].wait_recv()
-    for b in range(4):
-        for k in range(4):
-            part = ep[k, :, :, b * 256 : (b + 1) * 256].reshape(256, 256)
-            ep_t[b, :, k * 256 : (k + 1) * 256] = part.T
+    for h in range(2):
+        for b in range(4):
+            for k in range(4):
+                part = ep[h, k, :, :, b * 256 : (b + 1) * 256].reshape(256, 256)
+                ep_t[h, b, :, k * 256 : (k + 1) * 256] = part.T
 
     gn_pair.wait_recv()
 
@@ -376,6 +461,8 @@
     for copy in gn_x:
         copy.start()
 
+    if STOP == 11:
+        return finish()
     @pl.loop(0, 8)
     def _(i):
         rows = pl.ds(pl.multiple_of(i * 512, 512), 512)
@@ -390,26 +477,33 @@
     ge_pair = remote(ge_t.at[other], ge_sib, ge_ss.at[0], ge_rs.at[0], sib)
     ge_pair.start()
 
+    if STOP == 12:
+        return finish()
     gy_c = []
 
-    def scatter_y(h):
+    def scatter(h):
         for copy in gz_c[h]:
             copy.wait_recv()
         every = g_all[h].reshape(1024, 512)
+        here = reduce_me[h]
         copies = []
         for s in (2, 1, 3):
-            gw_s[h, s - 1] = dot(ep_t[add4(y, s)], every).astype(BF)
+            gw_s[h, s - 1] = dot(ep_t[h, add4(here, s)], every).astype(BF)
             copy = remote(
-                gw_s.at[h, s - 1], gw_r.at[h, s - 1], gy_ss.at[h, s - 1], gy_rs.at[h, s - 1], at_y(s)
+                gw_s.at[h, s - 1],
+                gw_r.at[h, s - 1],
+                gy_ss.at[h, s - 1],
+                gy_rs.at[h, s - 1],
+                reduce_at[h](s),
             )
             copy.start()
             copies.append(copy)
-        own = dot(ep_t[y], every)
+        own = dot(ep_t[h, here], every)
         gwk_ref[:, h * DH : (h + 1) * DH] = own[:, 0:256]
         gwv_ref[:, h * DH : (h + 1) * DH] = own[:, 256:512]
         gy_c.append(copies)
 
-    scatter_y(0)
+    scatter(0)
 
     ge_pair.wait_recv()
 
@@ -424,7 +518,18 @@
     for copy in ge_x:
         copy.start()
 
-    scatter_y(1)
+    if STOP == 13:
+        return finish()
+    scatter(1)
+
+    if STOP == 14:
+        return finish()
+    outs = [
+        pltpu.make_async_copy(src, dst, out_sem.at[i])
+        for i, (src, dst) in enumerate(
+            [(gd_ref, gd_hbm), (ge_ref, ge_hbm), (gwk_ref, gwk_hbm), (gwv_ref, gwv_hbm)]
+        )
+    ]
 
     for copy in rd_c:
         copy.wait_recv()
@@ -438,10 +543,11 @@
     total = gn_s[x].astype(F32)
     for s in range(3):
         total = total + gn_r[s].astype(F32)
-    scaled = total * gain_ref[:, share].astype(F32)
+    scaled = total * gain_ref[share].astype(F32).reshape(1, 512)
     rms = rms_v[:, 0:1]
     unit = dec_v[:, share].astype(F32) / rms
     gd_ref[...] = ((scaled - unit * inner[:, 0:1]) / rms).astype(BF)
+    outs[0].start()
 
     for copy in ge_x:
         copy.wait_recv()
@@ -449,6 +555,7 @@
     for s in range(3):
         total = total + ge_r[s].astype(F32)
     ge_ref[...] = total.astype(BF)
+    outs[1].start()
 
     for h in range(2):
         columns = slice(h * DH, (h + 1) * DH)
@@ -458,27 +565,18 @@
         gwk_ref[:, columns] = gwk_ref[:, columns] + total[:, 0:256]
         gwv_ref[:, columns] = gwv_ref[:, columns] + total[:, 256:512]
 
-    for copy in (
-        list(enc_x.values())
-        + list(enc_f.values())
-        + info_c
-        + epz
-        + list(ep_x.values())
-        + list(ep_f.values())
-        + kv_c[0]
-        + kv_c[1]
-        + ret_c[0]
-        + ret_c[1]
-        + rd_c
-        + gz_c[0]
-        + gz_c[1]
-        + [gn_pair, ge_pair]
-        + gn_x
-        + ge_x
-        + gy_c[0]
-        + gy_c[1]
-    ):
-        copy.wait_send()
+    outs[2].start()
+    outs[3].start()
+    finish()
+    for copy in outs:
+        copy.wait()
+
+
+def hand_on(a, b, c, d, a_out, b_out, c_out, d_out):
+    a_out[...] = a[...]
+    b_out[...] = b[...]
+    c_out[...] = c[...]
+    d_out[...] = d[...]
 
 
 def local(
@@ -494,24 +592,28 @@
     w_out,
     grad_out,
 ):
-    info = jnp.tile(jnp.stack([enc_owner, enc_example]), (4, 8))
     vmem = pl.BlockSpec(memory_space=pltpu.VMEM)
     smem = pl.BlockSpec(memory_space=pltpu.SMEM)
     hbm = pl.BlockSpec(memory_space=pl.ANY)
     dma = pltpu.SemaphoreType.DMA
     V = pltpu.VMEM
-    return pl.pallas_call(
+    shapes = (
+        jax.ShapeDtypeStruct((256, 512), BF),
+        jax.ShapeDtypeStruct((32, D), BF),
+        jax.ShapeDtypeStruct((256, 512), F32),
+        jax.ShapeDtypeStruct((256, 512), F32),
+    )
+    results = pl.pallas_call(
         kernel,
         name="cross_attention_grads",
-        out_shape=(
-            jax.ShapeDtypeStruct((256, 512), BF),
-            jax.ShapeDtypeStruct((32, D), BF),
-            jax.ShapeDtypeStruct((256, 512), F32),
-            jax.ShapeDtypeStruct((256, 512), F32),
-        ),
-        in_specs=[vmem, vmem, smem, vmem] + [hbm] * 6,
-        out_specs=(vmem,) * 4,
+        out_shape=shapes,
+        in_specs=[vmem, smem, smem, smem, vmem] + [hbm] * 6,
+        out_specs=(hbm,) * 4,
         scratch_shapes=[
+            V((256, 512), BF),
+            V((32, D), BF),
+            V((256, 512), F32),
+            V((256, 512), F32),
             V((256, D), BF),
             V((256, D), BF),
             V((D, 512), BF),
@@ -534,8 +636,8 @@
             V((2, 16, 32, 512), BF),
             V((2, 256, 512), BF),
             V((2, 4, 256, 512), BF),
-            V((4, 8, 32, 1024), BF),
-            V((4, 256, 1024), BF),
+            V((2, 4, 8, 32, 1024), BF),
+            V((2, 4, 256, 1024), BF),
             V((2, 3, 256, 512), BF),
             V((2, 3, 256, 512), BF),
             V((4, 2, 256, 512), BF),
@@ -548,12 +650,13 @@
             V((3, 32, D), BF),
             V((8, 8, 256), F32),
             dma((6,)),
+            dma((4,)),
             dma((8,)),
             dma((8,)),
             dma((7,)),
             dma((7,)),
-            dma((12,)),
-            dma((12,)),
+            dma((15,)),
+            dma((15,)),
             dma((8,)),
             dma((8,)),
             dma((2, 15)),
@@ -576,9 +679,10 @@
         ),
     )(
         enc,
-        info,
+        enc_owner,
+        enc_example,
         dec_lengths,
-        norm_gain.reshape(1, D),
+        norm_gain,
         dec,
         grad_out,
         w_query,
@@ -586,6 +690,13 @@
         w_value,
         w_out,
     )
+    return pl.pallas_call(
+        hand_on,
+        name="hand_on",
+        out_shape=shapes,
+        in_specs=[vmem] * 4,
+        out_specs=(vmem,) * 4,
+    )(*results)
 
 
 def solution(mesh):

time: 111 us -> 93.1 us (0.84)
  the two profiles are of different devices: /device:TPU:96 before, /device:TPU:1 now
where the time goes in v2:
time: 93.1 us; the launch traced here: 92.5 us
  Pallas kernels  91.8 us (99%)
    pallas_call x1, Pallas kernels, local(): pl.pallas_call(kernel, name='cross_attention_grads', out_shape=shapes, in...  89.3 us
    pallas_call x1, Pallas kernels, local(): pl.pallas_call(hand_on, name='hand_on', out_shape=shapes, in_specs=[vmem]...  2.52 us

profile of v2, /device:TPU:1, one launch (start us, length us, event | category | flops | bytes accessed | tf_op | source)
XLA Modules:
  0.0 92.5 jit_solution(5262613623856846115)
XLA Ops:
  0.6 89.3 %cross_attention_grads.1 = (bf16[256,512]{1,0:T(8,128)(2,1)}, bf16[32,4096]{1,0:T(8,128)(2,1)}, f32[256,512]{1,0:T(8,128)}, f32[256,512]{1,0:T(8,128)}) custom-call(bf16[32,4096]{1,0:T(8,128)(2,1)} %enc_ref.1, s32[32]{0:T(128)} %owner_ref.1, s32[32]{0:T(128)} %example_ref.1, s32[1,8]{1,0:T(1,128)} %len_ref.1, bf16[4096]{0:T(1024)(128)(2,1)} %gain_ref.1, ...), custom_call_target="tpu_custom_call" | custom-call | tf_op jit(solution)/shard_map/cross_attention_grads/pallas_call | solution.py:606
  90.0 2.5 %hand_on.1 = (bf16[256,512]{1,0:T(8,128)(2,1)}, bf16[32,4096]{1,0:T(8,128)(2,1)}, f32[256,512]{1,0:T(8,128)}, f32[256,512]{1,0:T(8,128)}) custom-call(bf16[256,512]{1,0:T(8,128)(2,1)} %get-tuple-element.8.a, bf16[32,4096]{1,0:T(8,128)(2,1)} %get-tuple-element.9.b, f32[256,512]{1,0:T(8,128)} %get-tuple-element.10.c, f32[256,512]{1,0:T(8,128)} %get-tuple-element.11.d), custom_call_target="tpu_custom_call" | custom-call | tf_op jit(solution)/shard_map/hand_on/pallas_call | solution.py:693

commit v3 on v2

v3 whole, which is shorter than its diff:
```python
import functools

import jax
import jax.numpy as jnp
from jax import lax
from jax.experimental import pallas as pl
from jax.experimental.pallas import tpu as pltpu
from jax.sharding import PartitionSpec as P

MESH = pl.DeviceIdType.MESH
BF = jnp.bfloat16
F32 = jnp.float32
DH = 256
D = 4096
NT = (((1,), (1,)), ((), ()))
TN = (((0,), (0,)), ((), ()))


def dot(a, b):
    return jnp.dot(a, b, preferred_element_type=F32)


def dot_nt(a, b):
    return lax.dot_general(a, b, NT, preferred_element_type=F32)


def dot_tn(a, b):
    return lax.dot_general(a, b, TN, preferred_element_type=F32)


class Copy:
    def __init__(self, copy, started):
        self.copy, self.started, self.received = copy, started, False

    def start(self):
        self.started.append(self)
        self.copy.start()

    def wait_recv(self):
        if not self.received:
            self.received = True
            self.copy.wait_recv()


def add4(value, step):
    return lax.rem(value + step, 4)


def kernel(
    enc_ref,
    owner_ref,
    example_ref,
    len_ref,
    gain_ref,
    dec_hbm,
    go_hbm,
    wq_hbm,
    wk_hbm,
    wv_hbm,
    wo_hbm,
    gd_hbm,
    ge_hbm,
    gwk_hbm,
    gwv_hbm,
    gd_ref,
    ge_ref,
    gwk_ref,
    gwv_ref,
    dec_v,
    go_v,
    wq_v,
    wk_v,
    wv_v,
    wo_v,
    enc_all,
    normed,
    rms_v,
    info_all,
    q_v,
    gc_v,
    gq_v,
    perm_v,
    place_t,
    one_s,
    one_b,
    one_r,
    ex_s,
    ex_r,
    kv_s,
    kv_r,
    key_v,
    value_v,
    ret_s,
    ret_r,
    g_own,
    g_all,
    ep,
    ep_t,
    gw_s,
    gw_r,
    gw_q,
    gn_t,
    gn_sib,
    gn_s,
    gn_r,
    gn_q,
    ge_t,
    ge_sib,
    ge_s,
    ge_r,
    ge_q,
    back_s,
    back_r,
    rd_all,
    load_sem,
    out_sem,
    one_ss,
    one_rs,
    enc_ss,
    enc_rs,
    eno_ss,
    eno_rs,
    ex_ss,
    ex_rs,
    info_ss,
    info_rs,
    epz_ss,
    epz_rs,
    ep_ss,
    ep_rs,
    kv_ss,
    kv_rs,
    ret_ss,
    ret_rs,
    rd_ss,
    rd_rs,
    gn_ss,
    gn_rs,
    ge_ss,
    ge_rs,
    gz_ss,
    gz_rs,
    gy_ss,
    gy_rs,
    back_ss,
    back_rs,
):
    dp = lax.axis_index("dp")
    mp = lax.axis_index("mp")
    y, z = dp // 4, lax.rem(dp, 4)
    x, c = mp // 2, lax.rem(mp, 2)
    other = 1 - c
    sib = (dp, x * 2 + other)

    def at_x(step):
        return (dp, add4(x, step) * 2 + c)

    def at_y(step):
        return (add4(y, step) * 4 + z, mp)

    def at_z(step):
        return (y * 4 + add4(z, step), mp)

    dp_peers = [(lax.rem(dp + i, 16), mp) for i in range(1, 16)]
    mp_peers = [(dp, lax.rem(mp + i, 8)) for i in range(1, 8)]

    started = []

    def remote(src, dst, ss, rs, who):
        copy = pltpu.make_async_remote_copy(
            src_ref=src, dst_ref=dst, send_sem=ss, recv_sem=rs, device_id=who, device_id_type=MESH
        )
        return Copy(copy, started)

    def finish():
        for i in range(6):
            load(i)
        for copy in started:
            copy.wait_recv()
        for copy in started:
            copy.copy.wait_send()

    class Gather:
        def __init__(self, src, slot, halves, place, at, ss, rs):
            self.slot, self.halves, self.place, self.at, self.ss, self.rs = slot, halves, place, at, ss, rs
            self.one = [remote(src, slot(place), ss.at[i], rs.at[i], at(s)) for i, s in enumerate((1, 3))]
            for copy in self.one:
                copy.start()

        def relay(self):
            self.two = []
            for i, s in enumerate((1, 3)):
                self.one[i].wait_recv()
                half = self.halves(self.slot(add4(self.place, 4 - s)))[i]
                copy = remote(half, half, self.ss.at[2 + i], self.rs.at[2 + i], self.at(s))
                copy.start()
                self.two.append(copy)

        def wait(self):
            for copy in self.two:
                copy.wait_recv()

    class Reduce:
        def __init__(self, term, halves, far, got, at, ss, rs):
            self.term, self.halves, self.far, self.got = term, halves, far, got
            self.at, self.ss, self.rs = at, ss, rs
            self.copies = []

        def send(self, src, dst, i, s):
            copy = remote(src, dst, self.ss.at[i], self.rs.at[i], self.at(s))
            copy.start()
            self.copies.append(copy)

        def send_far(self):
            for i, s in enumerate((1, 3)):
                self.send(self.halves(self.term(2))[i], self.far.at[i], i, s)

        def send_near(self):
            for i, s in enumerate((1, 3)):
                self.send(self.halves(self.term(s))[1 - i], self.halves(self.got.at[i])[1 - i], 2 + i, s)

        def relay(self):
            for i, s in enumerate((1, 3)):
                self.copies[i].wait_recv()
                half = self.halves(self.term(s))[i]
                half[...] = (half[...].astype(F32) + self.far[i].astype(F32)).astype(BF)
                self.send(half, self.halves(self.got.at[i])[i], 4 + i, s)

        def total(self, own):
            for copy in self.copies:
                copy.wait_recv()
            return own + self.got[0].astype(F32) + self.got[1].astype(F32)

    loads = [
        pltpu.make_async_copy(src, dst, load_sem.at[i])
        for i, (src, dst) in enumerate(
            [
                (dec_hbm, dec_v),
                (wq_hbm, wq_v),
                (go_hbm, go_v),
                (wo_hbm, wo_v),
                (wk_hbm, wk_v),
                (wv_hbm, wv_v),
            ]
        )
    ]
    loads[0].start()
    loaded = set()

    def load(i):
        if i not in loaded:
            loaded.add(i)
            loads[i].wait()

    barrier = pltpu.get_barrier_semaphore()
    for peer in dp_peers + mp_peers:
        pl.semaphore_signal(barrier, inc=1, device_id=peer, device_id_type=MESH)

    line = lax.broadcasted_iota(jnp.int32, (8, 128), 0)
    lane = lax.broadcasted_iota(jnp.int32, (8, 128), 1)
    ids = jnp.full((8, 128), -1, jnp.int32)
    for r in range(32):
        ids = jnp.where(lane == r, jnp.where(line == 0, owner_ref[r], example_ref[r]), ids)
    ids = ids.astype(F32)
    owner = ids[0:1, :]
    example = ids[1:2, :] + 1.0
    before = lax.broadcasted_iota(jnp.int32, (128, 128), 0)
    after = lax.broadcasted_iota(jnp.int32, (128, 128), 1)
    upper = jnp.where(before < after, 1.0, 0.0).astype(BF)
    onehot = lax.broadcasted_iota(jnp.int32, (16, 128), 0).astype(F32) == owner
    onehot = jnp.where(onehot, 1.0, 0.0)
    rank = jnp.sum(dot(onehot.astype(BF), upper) * onehot, axis=0, keepdims=True)
    later = jnp.where(rank > 0.5, 1.0, 0.0)
    order = dot(jnp.broadcast_to(later, (16, 128)).astype(BF), upper)[0:1, :]
    position = jnp.where(rank > 0.5, 16.0 + order, owner)
    perm = lax.broadcasted_iota(jnp.int32, (32, 128), 0).astype(F32) == position
    perm = jnp.where(perm, 1.0, 0.0)
    perm_v[...] = perm
    perm = perm[:, 0:32].astype(BF)
    lane_of = jnp.where(rank > 0.5, order + (mp * 16).astype(F32), -1.0)
    moved = jnp.broadcast_to(lane_of, (128, 128)).T == after.astype(F32)
    moved = jnp.where(moved, 1.0, 0.0).astype(BF)
    facts = jnp.where(line == 0, owner, jnp.where(line == 1, rank, example))
    facts = jnp.concatenate([facts, facts], axis=0).astype(BF)
    info_all[mp] = dot(facts, moved)[0:8, :]
    first = jnp.sum(perm_v[0:16, :] * example, axis=1, keepdims=True)
    for i in range(8):
        columns = slice(i * 512, (i + 1) * 512)
        rows = dot(perm, enc_ref[:, columns])
        enc_all[mp, 16:32, columns] = rows[16:32, :].astype(BF)
        one_s[:, i * 4 : (i + 1) * 4, :] = rows[0:16, :].reshape(16, 4, 128)
    one_s[:, 32:48, :] = jnp.broadcast_to(first.reshape(16, 1, 1), (16, 16, 128))
    one_b[...] = one_s[...].astype(BF)

    pl.semaphore_wait(barrier, 22)

    def later_halves(block):
        return block.at[:, 0 : D // 2], block.at[:, D // 2 : D]

    mine = enc_all.at[mp, 16:32, 0:D]
    later_g = Gather(
        mine, lambda place: enc_all.at[place * 2 + c, 16:32, 0:D], later_halves, x, at_x, enc_ss, enc_rs
    )
    one_c = [
        remote(one_b.at[peer[0]], one_r.at[dp], one_ss.at[i], one_rs.at[i], peer)
        for i, peer in enumerate(dp_peers)
    ]
    for copy in one_c:
        copy.start()
    one_r[dp] = one_b[dp]
    info_c = [
        remote(info_all.at[mp], info_all.at[mp], info_ss.at[i], info_rs.at[i], peer)
        for i, peer in enumerate(mp_peers)
    ]
    for copy in info_c:
        copy.start()

    def enc_forward(s):
        block = enc_all.at[add4(x, 4 - s) * 2 + c, 16:32, 0:D]
        return remote(block, block, enc_ss.at[4 + s], enc_rs.at[4 + s], sib)

    enc_f = {s: enc_forward(s) for s in range(4)}
    enc_f[0].start()

    for copy in loads[1:]:
        copy.start()

    load(0)

    @pl.loop(0, 8)
    def _(i):
        rows = pl.ds(pl.multiple_of(i * 32, 32), 32)
        wide = dec_v[rows, :].astype(F32)
        rms = jnp.sqrt(jnp.mean(wide * wide, axis=-1, keepdims=True) + 1e-06)
        rms_v[rows, :] = jnp.broadcast_to(rms, (32, 128))
        normed[rows, :] = ((wide * (1.0 / rms)) * gain_ref[...].astype(F32).reshape(1, D)).astype(BF)

    later_g.relay()
    for s in (1, 3):
        enc_f[s].start()
    for copy in one_c:
        copy.wait_recv()
    rows = one_r[...].astype(F32)
    enc_all[mp, 0:16, 0:D] = rows[:, 0:32, :].reshape(16, D).astype(BF)
    enc_all[mp, 0:16, D : D + 128] = rows[:, 32, :].astype(BF)
    def first_halves(block):
        return block.at[:, 0 : D // 2], block.at[:, D // 2 : D + 128]

    first_g = Gather(
        enc_all.at[mp, 0:16, :],
        lambda place: enc_all.at[place * 2 + c, 0:16, :],
        first_halves,
        x,
        at_x,
        eno_ss,
        eno_rs,
    )

    def eno_forward(s):
        block = enc_all.at[add4(x, 4 - s) * 2 + c, 0:16, :]
        return remote(block, block, eno_ss.at[4 + s], eno_rs.at[4 + s], sib)

    eno_f = {s: eno_forward(s) for s in range(4)}
    eno_f[0].start()
    epz = []
    for s in (1, 2, 3):
        for b in range(4):
            column = pl.multiple_of((b * 4 + add4(z, s)) * 256, 256)
            epz.append(
                remote(
                    enc_all.at[mp, :, pl.ds(column, 256)],
                    ep.at[0, z, mp, :, pl.ds(b * 256, 256)],
                    epz_ss.at[(s - 1) * 4 + b],
                    epz_rs.at[(s - 1) * 4 + b],
                    at_z(s),
                )
            )
        column = pl.multiple_of(add4(y, s) * 1024, 1024)
        epz.append(
            remote(
                enc_all.at[mp, :, pl.ds(column, 1024)],
                ep.at[1, y, mp],
                epz_ss.at[11 + s],
                epz_rs.at[11 + s],
                at_y(s),
            )
        )
    for copy in epz:
        copy.start()
    for b in range(4):
        column = pl.multiple_of((b * 4 + z) * 256, 256)
        ep[0, z, mp, :, pl.ds(b * 256, 256)] = enc_all[mp, :, pl.ds(column, 256)]
    ep[1, y, mp] = enc_all[mp, :, pl.ds(pl.multiple_of(y * 1024, 1024), 1024)]

    load(1)
    for h in range(2):
        q_v[h] = dot(normed[...], wq_v[:, h * DH : (h + 1) * DH]).astype(BF)
    def gc_and_first():
        load(2)
        load(3)
        for h in range(2):
            gc_v[h] = dot_nt(go_v[...], wo_v[h * DH : (h + 1) * DH, :]).astype(BF)
        for s in range(4):
            eno_f[s].wait_recv()
        rows = enc_all[:, 0:16, 0:D].reshape(128, D)
        for h in range(2):
            columns = slice(h * DH, (h + 1) * DH)
            key_v[h, 0:128, :] = dot(rows, wk_v[:, columns]).astype(BF)
            value_v[h, 0:128, :] = dot(rows, wv_v[:, columns]).astype(BF)

    first_g.relay()
    for s in (1, 3):
        eno_f[s].start()

    for copy in info_c:
        copy.wait_recv()
    info = info_all[0]
    for i in range(1, 8):
        info = info + info_all[i]
    block = lax.shift_right_logical(lax.broadcasted_iota(jnp.int32, (1, 128), 1), 4).astype(F32)
    target = info[0:1, :] * 24.0 + block * 3.0 + info[1:2, :] - 1.0
    slot_id = lax.broadcasted_iota(jnp.int32, (384, 128), 0).astype(F32)
    placed = jnp.where(slot_id == target, 1.0, 0.0)
    place = placed.astype(BF)
    place_t[...] = placed.T.astype(BF)
    slot_example = jnp.sum(placed * info[2:3, :], axis=1, keepdims=True)
    slot_example = jnp.broadcast_to(slot_example, (384, 128)).reshape(16, 24, 128)
    ex_s[...] = jnp.concatenate([slot_example, jnp.zeros((16, 8, 128), F32)], axis=1).astype(BF)
    ex_c = [
        remote(ex_s.at[peer[0]], ex_r.at[dp], ex_ss.at[i], ex_rs.at[i], peer)
        for i, peer in enumerate(dp_peers)
    ]
    for copy in ex_c:
        copy.start()
    ex_r[dp] = ex_s[dp]

    later_g.wait()
    enc_f[2].start()
    for s in range(4):
        enc_f[s].wait_recv()
    load(4)
    load(5)
    kv_c = []
    for h in range(2):
        columns = slice(h * DH, (h + 1) * DH)
        rows = enc_all[:, 16:32, 0:D].reshape(128, D)
        key = dot(place, dot(rows, wk_v[:, columns]).astype(BF)).reshape(16, 24, 256)
        value = dot(place, dot(rows, wv_v[:, columns]).astype(BF)).reshape(16, 24, 256)
        kv_s[h] = jnp.concatenate([key, value], axis=1).astype(BF)
        copies = [
            remote(kv_s.at[h, peer[0]], kv_r.at[h, dp], kv_ss.at[h, i], kv_rs.at[h, i], peer)
            for i, peer in enumerate(dp_peers)
        ]
        for copy in copies:
            copy.start()
        kv_r[h, dp] = kv_s[h, dp]
        kv_c.append(copies)

    first_g.wait()
    eno_f[2].start()
    for copy in epz:
        copy.wait_recv()
    ep_g = Gather(
        ep.at[:, :, mp],
        lambda place: ep.at[:, :, place * 2 + c],
        lambda block: (block.at[0], block.at[1]),
        x,
        at_x,
        ep_ss,
        ep_rs,
    )

    def ep_forward(s):
        block = ep.at[:, :, add4(x, 4 - s) * 2 + c]
        return remote(block, block, ep_ss.at[4 + s], ep_rs.at[4 + s], sib)

    ep_f = {s: ep_forward(s) for s in range(4)}
    ep_f[0].start()

    gc_and_first()

    place_of = lax.broadcasted_iota(jnp.int32, (1, 256), 1)
    bound = jnp.int32(0)
    segment = jnp.zeros((1, 256), jnp.int32)
    for e in range(8):
        bound = bound + len_ref[0, e]
        segment = segment + jnp.where(bound <= place_of, 1, 0)
    segment = segment.astype(F32) + 1.0

    scale = DH**-0.5
    ret_c = []
    gz_g = [[], []]
    gather_at, reduce_at = [at_z, at_y], [at_y, at_z]
    gather_me, reduce_me = [z, y], [y, z]

    def gather(h, part):
        here = gather_me[h]
        g_all[h, here, :, part] = g_own[h, :, part]
        gz_g[h].append(
            Gather(
                g_own.at[h, :, part],
                lambda place: g_all.at[h, place, :, part],
                lambda block: (block.at[0:4], block.at[4:8]),
                here,
                gather_at[h],
                gz_ss.at[h, part],
                gz_rs.at[h, part],
            )
        )

    row_dot = jnp.zeros((1, 256), F32)
    for copy in ex_c:
        copy.wait_recv()
    ex = enc_all[:, 0:16, D : D + 128].reshape(128, 128).astype(F32)
    ex = jnp.concatenate([ex, ex_r[...].astype(F32)[:, 0:24, :].reshape(384, 128)], axis=0)
    allowed = jnp.concatenate([ex, ex], axis=1) == segment
    for h in range(2):
        for copy in kv_c[h]:
            copy.wait_recv()
        both = kv_r[h].astype(F32)
        key_v[h, 128:512, :] = both[:, 0:24, :].reshape(384, 256).astype(BF)
        value_v[h, 128:512, :] = both[:, 24:48, :].reshape(384, 256).astype(BF)
        key = key_v[h]
        value = value_v[h]
        raw = dot_nt(key, q_v[h])
        scores = jnp.where(allowed, raw * scale, -1e30)
        top = jnp.max(scores, axis=0, keepdims=True)
        weights = jnp.where(allowed, jnp.exp(scores - top), 0.0)
        probs = weights / jnp.sum(weights, axis=0, keepdims=True)
        grad_probs = dot_nt(value, gc_v[h])
        inner = jnp.sum(probs * grad_probs, axis=0, keepdims=True)
        grad_scores = (probs * (grad_probs - inner) * scale).astype(BF)
        row_dot = row_dot + jnp.sum(grad_scores.astype(F32) * raw, axis=0, keepdims=True)
        grad_key = dot(grad_scores, q_v[h])
        grad_value = dot(probs.astype(BF), gc_v[h])
        ret_s[h] = jnp.concatenate(
            [grad_key[128:512, :].reshape(16, 24, 256), grad_value[128:512, :].reshape(16, 24, 256)],
            axis=1,
        ).astype(BF)
        copies = [
            remote(ret_s.at[h, peer[0]], ret_r.at[h, dp], ret_ss.at[h, i], ret_rs.at[h, i], peer)
            for i, peer in enumerate(dp_peers)
        ]
        for copy in copies:
            copy.start()
        ret_c.append(copies)
        ret_r[h, dp] = ret_s[h, dp]
        g_own[h, :, 0, :, 0:256] = grad_key[0:128, :].astype(BF).reshape(8, 16, 256)
        g_own[h, :, 0, :, 256:512] = grad_value[0:128, :].astype(BF).reshape(8, 16, 256)
        gather(h, 0)
        gq_v[:, h * DH : (h + 1) * DH] = dot_tn(grad_scores, key).astype(BF)

    rd_all[mp] = jnp.broadcast_to(row_dot, (8, 256))
    rd_c = [
        remote(rd_all.at[mp], rd_all.at[mp], rd_ss.at[i], rd_rs.at[i], peer)
        for i, peer in enumerate(mp_peers)
    ]
    for copy in rd_c:
        copy.start()

    def take_back(h):
        for copy in ret_c[h]:
            copy.wait_recv()
        both = ret_r[h].astype(F32)
        for k in range(2):
            back = both[:, k * 24 : (k + 1) * 24, :].reshape(384, 256).astype(BF)
            back = dot(place_t[...], back).astype(BF).reshape(8, 16, 256)
            g_own[h, :, 1, :, k * 256 : (k + 1) * 256] = back
        gather(h, 1)

    @pl.loop(0, 4)
    def _(i):
        for k in range(2):
            rows = pl.ds(pl.multiple_of((i * 2 + k) * 512, 512), 512)
            gn_t[i, k] = dot_nt(gq_v[...], wq_v[rows, :]).astype(BF)

    gn_pair = remote(gn_t.at[:, other], gn_sib, gn_ss.at[6], gn_rs.at[6], sib)
    gn_pair.start()

    ep_g.relay()
    for s in (1, 3):
        ep_f[s].start()
    for h in range(2):
        gz_g[h][0].relay()
    take_back(0)
    take_back(1)

    gn_pair.wait_recv()

    @pl.loop(0, 4)
    def _(i):
        gn_s[i] = (gn_t[i, c].astype(F32) + gn_sib[i].astype(F32)).astype(BF)

    def row_halves(block):
        return block.at[0:128], block.at[128:256]

    gn_red = Reduce(lambda s: gn_s.at[add4(x, s)], row_halves, gn_q, gn_r, at_x, gn_ss, gn_rs)
    gn_red.send_far()
    gn_red.send_near()

    @pl.loop(0, 8)
    def _(i):
        rows = pl.ds(pl.multiple_of(i * 512, 512), 512)
        total = jnp.zeros((256, 512), F32)
        for h in range(2):
            rows_h = g_own[h].reshape(256, 512)
            total = total + dot_nt(rows_h[:, 0:256], wk_v[rows, h * DH : (h + 1) * DH])
            total = total + dot_nt(rows_h[:, 256:512], wv_v[rows, h * DH : (h + 1) * DH])
        total = total.astype(BF).reshape(4, 2, 32, 512)
        for k in range(2):
            ge_t[k, :, :, rows] = total[:, k]

    ge_pair = remote(ge_t.at[other], ge_sib, ge_ss.at[6], ge_rs.at[6], sib)
    ge_pair.start()

    for h in range(2):
        gz_g[h][1].relay()

    ep_g.wait()
    ep_f[2].start()
    for s in range(4):
        ep_f[s].wait_recv()
    for h in range(2):
        for b in range(4):
            for k in range(4):
                part = ep[h, k, :, :, b * 256 : (b + 1) * 256].reshape(256, 256)
                ep_t[h, b, :, k * 256 : (k + 1) * 256] = part.T

    ge_pair.wait_recv()

    @pl.loop(0, 4)
    def _(i):
        ge_s[i] = (ge_t[c, i].astype(F32) + ge_sib[i].astype(F32)).astype(BF)

    ge_red = Reduce(
        lambda s: ge_s.at[add4(x, s)],
        lambda block: (block.at[0:16], block.at[16:32]),
        ge_q,
        ge_r,
        at_x,
        ge_ss,
        ge_rs,
    )
    ge_red.send_far()
    ge_red.send_near()
    gn_red.relay()

    gy_red = []

    def scatter(h):
        for g in gz_g[h]:
            g.wait()
        every = g_all[h].reshape(1024, 512)
        here = reduce_me[h]
        red = Reduce(
            lambda s: gw_s.at[h, s - 1],
            row_halves,
            gw_q.at[h],
            gw_r.at[h],
            reduce_at[h],
            gy_ss.at[h],
            gy_rs.at[h],
        )
        for s in (2, 1, 3):
            gw_s[h, s - 1] = dot(ep_t[h, add4(here, s)], every).astype(BF)
            if s == 2:
                red.send_far()
        red.send_near()
        own = dot(ep_t[h, here], every)
        gwk_ref[:, h * DH : (h + 1) * DH] = own[:, 0:256]
        gwv_ref[:, h * DH : (h + 1) * DH] = own[:, 256:512]
        gy_red.append(red)

    scatter(0)

    ge_red.relay()
    scatter(1)
    for red in gy_red:
        red.relay()

    outs = [
        pltpu.make_async_copy(src, dst, out_sem.at[i])
        for i, (src, dst) in enumerate(
            [(gd_ref, gd_hbm), (ge_ref, ge_hbm), (gwk_ref, gwk_hbm), (gwv_ref, gwv_hbm)]
        )
    ]

    for copy in rd_c:
        copy.wait_recv()
    inner = rd_all[0]
    for i in range(1, 8):
        inner = inner + rd_all[i]
    inner = jnp.broadcast_to(inner[0:1, :], (128, 256)).T * (1.0 / D)
    share = pl.ds(pl.multiple_of(mp * 512, 512), 512)
    total = gn_red.total(gn_s[x].astype(F32))
    scaled = total * gain_ref[share].astype(F32).reshape(1, 512)
    rms = rms_v[:, 0:1]
    unit = dec_v[:, share].astype(F32) / rms
    gd_ref[...] = ((scaled - unit * inner[:, 0:1]) / rms).astype(BF)
    outs[0].start()

    total = ge_red.total(ge_s[x].astype(F32))
    back_s[...] = total[0:16, :].reshape(16, 32, 128).astype(BF)
    back_c = [
        remote(back_s.at[peer[0]], back_r.at[dp], back_ss.at[i], back_rs.at[i], peer)
        for i, peer in enumerate(dp_peers)
    ]
    for copy in back_c:
        copy.start()
    back_r[dp] = back_s[dp]
    last = total[16:32, :].astype(BF)

    for h in range(2):
        columns = slice(h * DH, (h + 1) * DH)
        own = jnp.concatenate([gwk_ref[:, columns], gwv_ref[:, columns]], axis=1)
        total = gy_red[h].total(own)
        gwk_ref[:, columns] = total[:, 0:256]
        gwv_ref[:, columns] = total[:, 256:512]

    outs[2].start()
    outs[3].start()
    for copy in back_c:
        copy.wait_recv()
    rows = back_r[...].astype(F32).reshape(16, D).astype(BF)
    rows = jnp.concatenate([rows, last], axis=0)
    ge_ref[...] = dot_tn(perm_v[:, 0:32].astype(BF), rows).astype(BF)
    outs[1].start()
    finish()
    for copy in outs:
        copy.wait()


def hand_on(a, b, c, d, a_out, b_out, c_out, d_out):
    a_out[...] = a[...]
    b_out[...] = b[...]
    c_out[...] = c[...]
    d_out[...] = d[...]


def local(
    enc,
    enc_owner,
    enc_example,
    dec,
    dec_lengths,
    norm_gain,
    w_query,
    w_key,
    w_value,
    w_out,
    grad_out,
):
    vmem = pl.BlockSpec(memory_space=pltpu.VMEM)
    smem = pl.BlockSpec(memory_space=pltpu.SMEM)
    hbm = pl.BlockSpec(memory_space=pl.ANY)
    dma = pltpu.SemaphoreType.DMA
    V = pltpu.VMEM
    shapes = (
        jax.ShapeDtypeStruct((256, 512), BF),
        jax.ShapeDtypeStruct((32, D), BF),
        jax.ShapeDtypeStruct((256, 512), F32),
        jax.ShapeDtypeStruct((256, 512), F32),
    )
    results = pl.pallas_call(
        kernel,
        name="cross_attention_grads",
        out_shape=shapes,
        in_specs=[vmem, smem, smem, smem, vmem] + [hbm] * 6,
        out_specs=(hbm,) * 4,
        scratch_shapes=[
            V((256, 512), BF),
            V((32, D), BF),
            V((256, 512), F32),
            V((256, 512), F32),
            V((256, D), BF),
            V((256, D), BF),
            V((D, 512), BF),
            V((D, 512), BF),
            V((D, 512), BF),
            V((512, D), BF),
            V((8, 32, D + 128), BF),
            V((256, D), BF),
            V((256, 128), F32),
            V((8, 8, 128), F32),
            V((2, 256, 256), BF),
            V((2, 256, 256), BF),
            V((256, 512), BF),
            V((32, 128), F32),
            V((128, 384), BF),
            V((16, 48, 128), F32),
            V((16, 48, 128), BF),
            V((16, 48, 128), BF),
            V((16, 32, 128), BF),
            V((16, 32, 128), BF),
            V((2, 16, 48, 256), BF),
            V((2, 16, 48, 256), BF),
            V((2, 512, 256), BF),
            V((2, 512, 256), BF),
            V((2, 16, 48, 256), BF),
            V((2, 16, 48, 256), BF),
            V((2, 8, 2, 16, 512), BF),
            V((2, 4, 8, 2, 16, 512), BF),
            V((2, 4, 8, 32, 1024), BF),
            V((2, 4, 256, 1024), BF),
            V((2, 3, 256, 512), BF),
            V((2, 2, 256, 512), BF),
            V((2, 2, 128, 512), BF),
            V((4, 2, 256, 512), BF),
            V((4, 256, 512), BF),
            V((4, 256, 512), BF),
            V((2, 256, 512), BF),
            V((2, 128, 512), BF),
            V((2, 4, 32, D), BF),
            V((4, 32, D), BF),
            V((4, 32, D), BF),
            V((2, 32, D), BF),
            V((2, 16, D), BF),
            V((16, 32, 128), BF),
            V((16, 32, 128), BF),
            V((8, 8, 256), F32),
            dma((6,)),
            dma((4,)),
            dma((15,)),
            dma((15,)),
            dma((8,)),
            dma((8,)),
            dma((8,)),
            dma((8,)),
            dma((15,)),
            dma((15,)),
            dma((7,)),
            dma((7,)),
            dma((15,)),
            dma((15,)),
            dma((10,)),
            dma((10,)),
            dma((2, 15)),
            dma((2, 15)),
            dma((2, 15)),
            dma((2, 15)),
            dma((7,)),
            dma((7,)),
            dma((7,)),
            dma((7,)),
            dma((7,)),
            dma((7,)),
            dma((2, 2, 4)),
            dma((2, 2, 4)),
            dma((2, 6)),
            dma((2, 6)),
            dma((15,)),
            dma((15,)),
        ],
        compiler_params=pltpu.CompilerParams(
            collective_id=0, has_side_effects=True, vmem_limit_bytes=60 * 1024 * 1024
        ),
    )(
        enc,
        enc_owner,
        enc_example,
        dec_lengths,
        norm_gain,
        dec,
        grad_out,
        w_query,
        w_key,
        w_value,
        w_out,
    )
    return pl.pallas_call(
        hand_on,
        name="hand_on",
        out_shape=shapes,
        in_specs=[vmem] * 4,
        out_specs=(vmem,) * 4,
    )(*results)


def solution(mesh):
    placed = (
        P(("dp", "mp"), None),
        P(("dp", "mp")),
        P(("dp", "mp")),
        P("dp", None),
        P("dp", None),
        P(),
        P(None, "mp"),
        P(None, "mp"),
        P(None, "mp"),
        P("mp", None),
        P("dp", None),
    )
    return jax.shard_map(
        local,
        mesh=mesh,
        in_specs=placed,
        out_specs=(P("dp", "mp"), P(("dp", "mp"), None), P("dp", "mp"), P("dp", "mp")),
        check_vma=False,
    )
```

time: 93.1 us -> 82.8 us (0.89)
  Pallas kernels: 91.8 us -> 82 us
    pallas_call x1, Pallas kernels: 89.3 us -> 79.5 us  [local(): pl.pallas_call(kernel, name='cross_attention_grads', out_shape=shapes, in...]
where the time goes in v3:
time: 82.8 us; the launch traced here: 82.7 us
  Pallas kernels  82 us (99%)
    pallas_call x1, Pallas kernels, local(): pl.pallas_call(kernel, name='cross_attention_grads', out_shape=shapes, in...  79.5 us
    pallas_call x1, Pallas kernels, local(): pl.pallas_call(hand_on, name='hand_on', out_shape=shapes, in_specs=[vmem]...  2.52 us

profile of v3, /device:TPU:1, one launch (start us, length us, event | category | flops | bytes accessed | tf_op | source)
XLA Modules:
  0.0 82.7 jit_solution(9949240464367468453)
XLA Ops:
  0.6 79.5 %cross_attention_grads.1 = (bf16[256,512]{1,0:T(8,128)(2,1)}, bf16[32,4096]{1,0:T(8,128)(2,1)}, f32[256,512]{1,0:T(8,128)}, f32[256,512]{1,0:T(8,128)}) custom-call(bf16[32,4096]{1,0:T(8,128)(2,1)} %enc_ref.1, s32[32]{0:T(128)} %owner_ref.1, s32[32]{0:T(128)} %example_ref.1, s32[1,8]{1,0:T(1,128)} %len_ref.1, bf16[4096]{0:T(1024)(128)(2,1)} %gain_ref.1, ...), custom_call_target="tpu_custom_call" | custom-call | tf_op jit(solution)/shard_map/cross_attention_grads/pallas_call | solution.py:764
  80.2 2.5 %hand_on.1 = (bf16[256,512]{1,0:T(8,128)(2,1)}, bf16[32,4096]{1,0:T(8,128)(2,1)}, f32[256,512]{1,0:T(8,128)}, f32[256,512]{1,0:T(8,128)}) custom-call(bf16[256,512]{1,0:T(8,128)(2,1)} %get-tuple-element.8.a, bf16[32,4096]{1,0:T(8,128)(2,1)} %get-tuple-element.9.b, f32[256,512]{1,0:T(8,128)} %get-tuple-element.10.c, f32[256,512]{1,0:T(8,128)} %get-tuple-element.11.d), custom_call_target="tpu_custom_call" | custom-call | tf_op jit(solution)/shard_map/hand_on/pallas_call | solution.py:870

commit v4 on v3

--- a/solution.py
+++ b/solution.py
@@ -244,7 +244,8 @@
             ]
         )
     ]
-    loads[0].start()
+    for copy in loads:
+        copy.start()
     loaded = set()
 
     def load(i):
@@ -322,9 +323,6 @@
     enc_f = {s: enc_forward(s) for s in range(4)}
     enc_f[0].start()
 
-    for copy in loads[1:]:
-        copy.start()
-
     load(0)
 
     @pl.loop(0, 8)
@@ -392,9 +390,6 @@
         ep[0, z, mp, :, pl.ds(b * 256, 256)] = enc_all[mp, :, pl.ds(column, 256)]
     ep[1, y, mp] = enc_all[mp, :, pl.ds(pl.multiple_of(y * 1024, 1024), 1024)]
 
-    load(1)
-    for h in range(2):
-        q_v[h] = dot(normed[...], wq_v[:, h * DH : (h + 1) * DH]).astype(BF)
     def gc_and_first():
         load(2)
         load(3)
@@ -407,10 +402,6 @@
             columns = slice(h * DH, (h + 1) * DH)
             key_v[h, 0:128, :] = dot(rows, wk_v[:, columns]).astype(BF)
             value_v[h, 0:128, :] = dot(rows, wv_v[:, columns]).astype(BF)
-
-    first_g.relay()
-    for s in (1, 3):
-        eno_f[s].start()
 
     for copy in info_c:
         copy.wait_recv()
@@ -436,6 +427,9 @@
 
     later_g.wait()
     enc_f[2].start()
+    load(1)
+    for h in range(2):
+        q_v[h] = dot(normed[...], wq_v[:, h * DH : (h + 1) * DH]).astype(BF)
     for s in range(4):
         enc_f[s].wait_recv()
     load(4)
@@ -455,6 +449,10 @@
             copy.start()
         kv_r[h, dp] = kv_s[h, dp]
         kv_c.append(copies)
+        if h == 0:
+            first_g.relay()
+            for s in (1, 3):
+                eno_f[s].start()
 
     first_g.wait()
     eno_f[2].start()
@@ -568,6 +566,12 @@
             g_own[h, :, 1, :, k * 256 : (k + 1) * 256] = back
         gather(h, 1)
 
+    def row_halves(block):
+        return block.at[0:128], block.at[128:256]
+
+    def column_halves(block):
+        return block.at[:, 0 : D // 2], block.at[:, D // 2 : D]
+
     @pl.loop(0, 4)
     def _(i):
         for k in range(2):
@@ -577,47 +581,75 @@
     gn_pair = remote(gn_t.at[:, other], gn_sib, gn_ss.at[6], gn_rs.at[6], sib)
     gn_pair.start()
 
+    ge_pair = []
+
+    def enc_term(part):
+        @pl.loop(0, 8)
+        def _(i):
+            rows = pl.ds(pl.multiple_of(i * 512, 512), 512)
+            total = jnp.zeros((128, 512), F32)
+            for h in range(2):
+                own = g_own[h, :, part].reshape(128, 512)
+                total = total + dot_nt(own[:, 0:256], wk_v[rows, h * DH : (h + 1) * DH])
+                total = total + dot_nt(own[:, 256:512], wv_v[rows, h * DH : (h + 1) * DH])
+            total = total.astype(BF).reshape(4, 2, 16, 512)
+            for k in range(2):
+                ge_t[part, k, :, :, rows] = total[:, k]
+
+        pair = remote(
+            ge_t.at[part, other], ge_sib.at[part], ge_ss.at[part, 6], ge_rs.at[part, 6], sib
+        )
+        pair.start()
+        ge_pair.append(pair)
+
+    ge_red = []
+
+    def enc_reduce(part):
+        ge_pair[part].wait_recv()
+
+        @pl.loop(0, 4)
+        def _(i):
+            ge_s[part, i] = (ge_t[part, c, i].astype(F32) + ge_sib[part, i].astype(F32)).astype(BF)
+
+        red = Reduce(
+            lambda s: ge_s.at[part, add4(x, s)],
+            column_halves,
+            ge_q.at[part],
+            ge_r.at[part],
+            at_x,
+            ge_ss.at[part],
+            ge_rs.at[part],
+        )
+        red.send_far()
+        red.send_near()
+        ge_red.append(red)
+
     ep_g.relay()
     for s in (1, 3):
         ep_f[s].start()
-    for h in range(2):
-        gz_g[h][0].relay()
-    take_back(0)
-    take_back(1)
-
+    enc_term(0)
     gn_pair.wait_recv()
 
     @pl.loop(0, 4)
     def _(i):
         gn_s[i] = (gn_t[i, c].astype(F32) + gn_sib[i].astype(F32)).astype(BF)
 
-    def row_halves(block):
-        return block.at[0:128], block.at[128:256]
-
     gn_red = Reduce(lambda s: gn_s.at[add4(x, s)], row_halves, gn_q, gn_r, at_x, gn_ss, gn_rs)
     gn_red.send_far()
     gn_red.send_near()
-
-    @pl.loop(0, 8)
-    def _(i):
-        rows = pl.ds(pl.multiple_of(i * 512, 512), 512)
-        total = jnp.zeros((256, 512), F32)
-        for h in range(2):
-            rows_h = g_own[h].reshape(256, 512)
-            total = total + dot_nt(rows_h[:, 0:256], wk_v[rows, h * DH : (h + 1) * DH])
-            total = total + dot_nt(rows_h[:, 256:512], wv_v[rows, h * DH : (h + 1) * DH])
-        total = total.astype(BF).reshape(4, 2, 32, 512)
-        for k in range(2):
-            ge_t[k, :, :, rows] = total[:, k]
-
-    ge_pair = remote(ge_t.at[other], ge_sib, ge_ss.at[6], ge_rs.at[6], sib)
-    ge_pair.start()
-
+    for h in range(2):
+        gz_g[h][0].relay()
+    enc_reduce(0)
+    take_back(0)
+    take_back(1)
+    enc_term(1)
     for h in range(2):
         gz_g[h][1].relay()
-
     ep_g.wait()
     ep_f[2].start()
+    gn_red.relay()
+    enc_reduce(1)
+
     for s in range(4):
         ep_f[s].wait_recv()
     for h in range(2):
@@ -625,25 +657,7 @@
             for k in range(4):
                 part = ep[h, k, :, :, b * 256 : (b + 1) * 256].reshape(256, 256)
                 ep_t[h, b, :, k * 256 : (k + 1) * 256] = part.T
-
-    ge_pair.wait_recv()
-
-    @pl.loop(0, 4)
-    def _(i):
-        ge_s[i] = (ge_t[c, i].astype(F32) + ge_sib[i].astype(F32)).astype(BF)
-
-    ge_red = Reduce(
-        lambda s: ge_s.at[add4(x, s)],
-        lambda block: (block.at[0:16], block.at[16:32]),
-        ge_q,
-        ge_r,
-        at_x,
-        ge_ss,
-        ge_rs,
-    )
-    ge_red.send_far()
-    ge_red.send_near()
-    gn_red.relay()
+    ge_red[0].relay()
 
     gy_red = []
 
@@ -673,8 +687,8 @@
 
     scatter(0)
 
-    ge_red.relay()
     scatter(1)
+    ge_red[1].relay()
     for red in gy_red:
         red.relay()
 
@@ -684,6 +698,16 @@
             [(gd_ref, gd_hbm), (ge_ref, ge_hbm), (gwk_ref, gwk_hbm), (gwv_ref, gwv_hbm)]
         )
     ]
+
+    total = ge_red[0].total(ge_s[0, x].astype(F32))
+    back_s[...] = total.reshape(16, 32, 128).astype(BF)
+    back_c = [
+        remote(back_s.at[peer[0]], back_r.at[dp], back_ss.at[i], back_rs.at[i], peer)
+        for i, peer in enumerate(dp_peers)
+    ]
+    for copy in back_c:
+        copy.start()
+    back_r[dp] = back_s[dp]
 
     for copy in rd_c:
         copy.wait_recv()
@@ -699,17 +723,6 @@
     gd_ref[...] = ((scaled - unit * inner[:, 0:1]) / rms).astype(BF)
     outs[0].start()
 
-    total = ge_red.total(ge_s[x].astype(F32))
-    back_s[...] = total[0:16, :].reshape(16, 32, 128).astype(BF)
-    back_c = [
-        remote(back_s.at[peer[0]], back_r.at[dp], back_ss.at[i], back_rs.at[i], peer)
-        for i, peer in enumerate(dp_peers)
-    ]
-    for copy in back_c:
-        copy.start()
-    back_r[dp] = back_s[dp]
-    last = total[16:32, :].astype(BF)
-
     for h in range(2):
         columns = slice(h * DH, (h + 1) * DH)
         own = jnp.concatenate([gwk_ref[:, columns], gwv_ref[:, columns]], axis=1)
@@ -719,6 +732,7 @@
 
     outs[2].start()
     outs[3].start()
+    last = ge_red[1].total(ge_s[1, x].astype(F32)).astype(BF)
     for copy in back_c:
         copy.wait_recv()
     rows = back_r[...].astype(F32).reshape(16, D).astype(BF)
@@ -810,11 +824,11 @@
             V((4, 256, 512), BF),
             V((2, 256, 512), BF),
             V((2, 128, 512), BF),
-            V((2, 4, 32, D), BF),
-            V((4, 32, D), BF),
-            V((4, 32, D), BF),
-            V((2, 32, D), BF),
-            V((2, 16, D), BF),
+            V((2, 2, 4, 16, D), BF),
+            V((2, 4, 16, D), BF),
+            V((2, 4, 16, D), BF),
+            V((2, 2, 16, D), BF),
+            V((2, 2, 16, D // 2), BF),
             V((16, 32, 128), BF),
             V((16, 32, 128), BF),
             V((8, 8, 256), F32),
@@ -842,8 +856,8 @@
             dma((7,)),
             dma((7,)),
             dma((7,)),
-            dma((7,)),
-            dma((7,)),
+            dma((2, 7)),
+            dma((2, 7)),
             dma((2, 2, 4)),
             dma((2, 2, 4)),
             dma((2, 6)),

time: 82.8 us -> 75.7 us (0.914)
  Pallas kernels: 82 us -> 74.9 us
    pallas_call x1, Pallas kernels: 79.5 us -> 72.4 us  [local(): pl.pallas_call(kernel, name='cross_attention_grads', out_shape=shapes, in...]
where the time goes in v4:
time: 75.7 us; the launch traced here: 75.6 us
  Pallas kernels  74.9 us (99%)
    pallas_call x1, Pallas kernels, local(): pl.pallas_call(kernel, name='cross_attention_grads', out_shape=shapes, in...  72.4 us
    pallas_call x1, Pallas kernels, local(): pl.pallas_call(hand_on, name='hand_on', out_shape=shapes, in_specs=[vmem]...  2.52 us

profile of v4, /device:TPU:1, one launch (start us, length us, event | category | flops | bytes accessed | tf_op | source)
XLA Modules:
  0.0 75.6 jit_solution(131759298752825077)
XLA Ops:
  0.6 72.4 %cross_attention_grads.1 = (bf16[256,512]{1,0:T(8,128)(2,1)}, bf16[32,4096]{1,0:T(8,128)(2,1)}, f32[256,512]{1,0:T(8,128)}, f32[256,512]{1,0:T(8,128)}) custom-call(bf16[32,4096]{1,0:T(8,128)(2,1)} %enc_ref.1, s32[32]{0:T(128)} %owner_ref.1, s32[32]{0:T(128)} %example_ref.1, s32[1,8]{1,0:T(1,128)} %len_ref.1, bf16[4096]{0:T(1024)(128)(2,1)} %gain_ref.1, ...), custom_call_target="tpu_custom_call" | custom-call | tf_op jit(solution)/shard_map/cross_attention_grads/pallas_call | solution.py:778
  73.0 2.5 %hand_on.1 = (bf16[256,512]{1,0:T(8,128)(2,1)}, bf16[32,4096]{1,0:T(8,128)(2,1)}, f32[256,512]{1,0:T(8,128)}, f32[256,512]{1,0:T(8,128)}) custom-call(bf16[256,512]{1,0:T(8,128)(2,1)} %get-tuple-element.8.a, bf16[32,4096]{1,0:T(8,128)(2,1)} %get-tuple-element.9.b, f32[256,512]{1,0:T(8,128)} %get-tuple-element.10.c, f32[256,512]{1,0:T(8,128)} %get-tuple-element.11.d), custom_call_target="tpu_custom_call" | custom-call | tf_op jit(solution)/shard_map/hand_on/pallas_call | solution.py:884

commit v5 on v4

--- a/solution.py
+++ b/solution.py
@@ -47,7 +47,7 @@
 
 
 def kernel(
-    enc_ref,
+    enc_hbm,
     owner_ref,
     example_ref,
     len_ref,
@@ -66,6 +66,7 @@
     ge_ref,
     gwk_ref,
     gwv_ref,
+    enc_ref,
     dec_v,
     go_v,
     wq_v,
@@ -164,6 +165,10 @@
     dp_peers = [(lax.rem(dp + i, 16), mp) for i in range(1, 16)]
     mp_peers = [(dp, lax.rem(mp + i, 8)) for i in range(1, 8)]
 
+    barrier = pltpu.get_barrier_semaphore()
+    for peer in dp_peers + mp_peers:
+        pl.semaphore_signal(barrier, inc=1, device_id=peer, device_id_type=MESH)
+
     started = []
 
     def remote(src, dst, ss, rs, who):
@@ -173,7 +178,7 @@
         return Copy(copy, started)
 
     def finish():
-        for i in range(6):
+        for i in range(7):
             load(i)
         for copy in started:
             copy.wait_recv()
@@ -241,21 +246,18 @@
                 (wo_hbm, wo_v),
                 (wk_hbm, wk_v),
                 (wv_hbm, wv_v),
+                (enc_hbm, enc_ref),
             ]
         )
     ]
-    for copy in loads:
-        copy.start()
+    for i in (6, 0, 1, 4, 5, 2, 3):
+        loads[i].start()
     loaded = set()
 
     def load(i):
         if i not in loaded:
             loaded.add(i)
             loads[i].wait()
-
-    barrier = pltpu.get_barrier_semaphore()
-    for peer in dp_peers + mp_peers:
-        pl.semaphore_signal(barrier, inc=1, device_id=peer, device_id_type=MESH)
 
     line = lax.broadcasted_iota(jnp.int32, (8, 128), 0)
     lane = lax.broadcasted_iota(jnp.int32, (8, 128), 1)
@@ -285,6 +287,7 @@
     facts = jnp.concatenate([facts, facts], axis=0).astype(BF)
     info_all[mp] = dot(facts, moved)[0:8, :]
     first = jnp.sum(perm_v[0:16, :] * example, axis=1, keepdims=True)
+    load(6)
     for i in range(8):
         columns = slice(i * 512, (i + 1) * 512)
         rows = dot(perm, enc_ref[:, columns])
@@ -333,6 +336,9 @@
         rms_v[rows, :] = jnp.broadcast_to(rms, (32, 128))
         normed[rows, :] = ((wide * (1.0 / rms)) * gain_ref[...].astype(F32).reshape(1, D)).astype(BF)
 
+    load(1)
+    for h in range(2):
+        q_v[h] = dot(normed[...], wq_v[:, h * DH : (h + 1) * DH]).astype(BF)
     later_g.relay()
     for s in (1, 3):
         enc_f[s].start()
@@ -427,9 +433,6 @@
 
     later_g.wait()
     enc_f[2].start()
-    load(1)
-    for h in range(2):
-        q_v[h] = dot(normed[...], wq_v[:, h * DH : (h + 1) * DH]).astype(BF)
     for s in range(4):
         enc_f[s].wait_recv()
     load(4)
@@ -545,9 +548,10 @@
         ret_r[h, dp] = ret_s[h, dp]
         g_own[h, :, 0, :, 0:256] = grad_key[0:128, :].astype(BF).reshape(8, 16, 256)
         g_own[h, :, 0, :, 256:512] = grad_value[0:128, :].astype(BF).reshape(8, 16, 256)
+        gq_v[:, h * DH : (h + 1) * DH] = dot_tn(grad_scores, key).astype(BF)
+
+    for h in range(2):
         gather(h, 0)
-        gq_v[:, h * DH : (h + 1) * DH] = dot_tn(grad_scores, key).astype(BF)
-
     rd_all[mp] = jnp.broadcast_to(row_dot, (8, 256))
     rd_c = [
         remote(rd_all.at[mp], rd_all.at[mp], rd_ss.at[i], rd_rs.at[i], peer)
@@ -587,11 +591,10 @@
         @pl.loop(0, 8)
         def _(i):
             rows = pl.ds(pl.multiple_of(i * 512, 512), 512)
-            total = jnp.zeros((128, 512), F32)
-            for h in range(2):
-                own = g_own[h, :, part].reshape(128, 512)
-                total = total + dot_nt(own[:, 0:256], wk_v[rows, h * DH : (h + 1) * DH])
-                total = total + dot_nt(own[:, 256:512], wv_v[rows, h * DH : (h + 1) * DH])
+            own = [g_own[h, :, part].reshape(128, 512) for h in range(2)]
+            keys = jnp.concatenate([own[0][:, 0:256], own[1][:, 0:256]], axis=1)
+            values = jnp.concatenate([own[0][:, 256:512], own[1][:, 256:512]], axis=1)
+            total = dot_nt(keys, wk_v[rows, :]) + dot_nt(values, wv_v[rows, :])
             total = total.astype(BF).reshape(4, 2, 16, 512)
             for k in range(2):
                 ge_t[part, k, :, :, rows] = total[:, k]
@@ -637,11 +640,11 @@
     gn_red = Reduce(lambda s: gn_s.at[add4(x, s)], row_halves, gn_q, gn_r, at_x, gn_ss, gn_rs)
     gn_red.send_far()
     gn_red.send_near()
+    take_back(0)
+    enc_reduce(0)
+    take_back(1)
     for h in range(2):
         gz_g[h][0].relay()
-    enc_reduce(0)
-    take_back(0)
-    take_back(1)
     enc_term(1)
     for h in range(2):
         gz_g[h][1].relay()
@@ -688,9 +691,9 @@
     scatter(0)
 
     scatter(1)
-    ge_red[1].relay()
     for red in gy_red:
         red.relay()
+    ge_red[1].relay()
 
     outs = [
         pltpu.make_async_copy(src, dst, out_sem.at[i])
@@ -744,11 +747,18 @@
         copy.wait()
 
 
-def hand_on(a, b, c, d, a_out, b_out, c_out, d_out):
-    a_out[...] = a[...]
-    b_out[...] = b[...]
-    c_out[...] = c[...]
-    d_out[...] = d[...]
+def hand_on(a, b, c, d, a_out, b_out, c_out, d_out, a_v, b_v, c_v, d_v, sem):
+    into = [(c, c_v), (d, d_v), (a, a_v), (b, b_v)]
+    out = [(c_v, c_out), (d_v, d_out), (a_v, a_out), (b_v, b_out)]
+    into = [pltpu.make_async_copy(src, dst, sem.at[0, i]) for i, (src, dst) in enumerate(into)]
+    out = [pltpu.make_async_copy(src, dst, sem.at[1, i]) for i, (src, dst) in enumerate(out)]
+    for copy in into:
+        copy.start()
+    for first, second in zip(into, out):
+        first.wait()
+        second.start()
+    for copy in out:
+        copy.wait()
 
 
 def local(
@@ -779,13 +789,14 @@
         kernel,
         name="cross_attention_grads",
         out_shape=shapes,
-        in_specs=[vmem, smem, smem, smem, vmem] + [hbm] * 6,
+        in_specs=[hbm, smem, smem, smem, vmem] + [hbm] * 6,
         out_specs=(hbm,) * 4,
         scratch_shapes=[
             V((256, 512), BF),
             V((32, D), BF),
             V((256, 512), F32),
             V((256, 512), F32),
+            V((32, D), BF),
             V((256, D), BF),
             V((256, D), BF),
             V((D, 512), BF),
@@ -832,7 +843,7 @@
             V((16, 32, 128), BF),
             V((16, 32, 128), BF),
             V((8, 8, 256), F32),
-            dma((6,)),
+            dma((7,)),
             dma((4,)),
             dma((15,)),
             dma((15,)),
@@ -885,8 +896,9 @@
         hand_on,
         name="hand_on",
         out_shape=shapes,
-        in_specs=[vmem] * 4,
-        out_specs=(vmem,) * 4,
+        in_specs=[hbm] * 4,
+        out_specs=(hbm,) * 4,
+        scratch_shapes=[V(shape.shape, shape.dtype) for shape in shapes] + [dma((2, 4))],
     )(*results)
 
 

time: 75.7 us -> 74.9 us (0.989)
  Pallas kernels: 74.9 us -> 73.9 us
where the time goes in v5:
time: 74.9 us; the launch traced here: 74.7 us
  Pallas kernels  73.9 us (99%)
  between operations  0.8 us (1%)
    pallas_call x1, Pallas kernels, local(): pl.pallas_call(kernel, name='cross_attention_grads', out_shape=shapes, in...  71.7 us
    pallas_call x1, Pallas kernels, local(): pl.pallas_call(hand_on, name='hand_on', out_shape=shapes, in_specs=[hbm]...  2.25 us

profile of v5, /device:TPU:1, one launch (start us, length us, event | category | flops | bytes accessed | tf_op | source)
XLA Modules:
  0.0 74.7 jit_solution(15277917607828577088)
XLA Ops:
  0.6 71.7 %cross_attention_grads.1 = (bf16[256,512]{1,0:T(8,128)(2,1)}, bf16[32,4096]{1,0:T(8,128)(2,1)}, f32[256,512]{1,0:T(8,128)}, f32[256,512]{1,0:T(8,128)}) custom-call(bf16[32,4096]{1,0:T(8,128)(2,1)} %enc_hbm.1, s32[32]{0:T(128)} %owner_ref.1, s32[32]{0:T(128)} %example_ref.1, s32[1,8]{1,0:T(1,128)} %len_ref.1, bf16[4096]{0:T(1024)(128)(2,1)} %gain_ref.1, ...), custom_call_target="tpu_custom_call" | custom-call | tf_op jit(solution)/shard_map/cross_attention_grads/pallas_call | solution.py:788
  72.3 2.2 %hand_on.1 = (bf16[256,512]{1,0:T(8,128)(2,1)}, bf16[32,4096]{1,0:T(8,128)(2,1)}, f32[256,512]{1,0:T(8,128)}, f32[256,512]{1,0:T(8,128)}) custom-call(bf16[256,512]{1,0:T(8,128)(2,1)} %get-tuple-element.8.a, bf16[32,4096]{1,0:T(8,128)(2,1)} %get-tuple-element.9.b, f32[256,512]{1,0:T(8,128)} %get-tuple-element.10.c, f32[256,512]{1,0:T(8,128)} %get-tuple-element.11.d), custom_call_target="tpu_custom_call" | custom-call | tf_op jit(solution)/shard_map/hand_on/pallas_call | solution.py:895

commit v6 on v5

--- a/solution.py
+++ b/solution.py
@@ -698,7 +698,12 @@
     outs = [
         pltpu.make_async_copy(src, dst, out_sem.at[i])
         for i, (src, dst) in enumerate(
-            [(gd_ref, gd_hbm), (ge_ref, ge_hbm), (gwk_ref, gwk_hbm), (gwv_ref, gwv_hbm)]
+            [(gd_ref, gd_hbm), (ge_ref, ge_hbm)]
+            + [
+                (ref.at[:, h * DH : (h + 1) * DH], hbm.at[:, h * DH : (h + 1) * DH])
+                for h in range(2)
+                for ref, hbm in ((gwk_ref, gwk_hbm), (gwv_ref, gwv_hbm))
+            ]
         )
     ]
 
@@ -732,16 +737,17 @@
         total = gy_red[h].total(own)
         gwk_ref[:, columns] = total[:, 0:256]
         gwv_ref[:, columns] = total[:, 256:512]
-
-    outs[2].start()
-    outs[3].start()
-    last = ge_red[1].total(ge_s[1, x].astype(F32)).astype(BF)
-    for copy in back_c:
-        copy.wait_recv()
-    rows = back_r[...].astype(F32).reshape(16, D).astype(BF)
-    rows = jnp.concatenate([rows, last], axis=0)
-    ge_ref[...] = dot_tn(perm_v[:, 0:32].astype(BF), rows).astype(BF)
-    outs[1].start()
+        outs[2 + 2 * h].start()
+        outs[3 + 2 * h].start()
+        if h == 0:
+            last = ge_red[1].total(ge_s[1, x].astype(F32)).astype(BF)
+            for copy in back_c:
+                copy.wait_recv()
+            rows = back_r[...].astype(F32).reshape(16, D).astype(BF)
+            rows = jnp.concatenate([rows, last], axis=0)
+            ge_ref[...] = dot_tn(perm_v[:, 0:32].astype(BF), rows).astype(BF)
+            outs[1].start()
+
     finish()
     for copy in outs:
         copy.wait()
@@ -844,7 +850,7 @@
             V((16, 32, 128), BF),
             V((8, 8, 256), F32),
             dma((7,)),
-            dma((4,)),
+            dma((6,)),
             dma((15,)),
             dma((15,)),
             dma((8,)),

time: 74.9 us -> 75.1 us (level)
  no operation moved by 1% of the time
where the time goes in v6:
time: 75.1 us; the launch traced here: 75 us
  Pallas kernels  74.2 us (99%)
  between operations  0.8 us (1%)
    pallas_call x1, Pallas kernels, local(): pl.pallas_call(kernel, name='cross_attention_grads', out_shape=shapes, in...  71.9 us
    pallas_call x1, Pallas kernels, local(): pl.pallas_call(hand_on, name='hand_on', out_shape=shapes, in_specs=[hbm]...  2.25 us

profile of v6, /device:TPU:1, one launch (start us, length us, event | category | flops | bytes accessed | tf_op | source)
XLA Modules:
  0.0 75.0 jit_solution(2007603615594179811)
XLA Ops:
  0.6 71.9 %cross_attention_grads.1 = (bf16[256,512]{1,0:T(8,128)(2,1)}, bf16[32,4096]{1,0:T(8,128)(2,1)}, f32[256,512]{1,0:T(8,128)}, f32[256,512]{1,0:T(8,128)}) custom-call(bf16[32,4096]{1,0:T(8,128)(2,1)} %enc_hbm.1, s32[32]{0:T(128)} %owner_ref.1, s32[32]{0:T(128)} %example_ref.1, s32[1,8]{1,0:T(1,128)} %len_ref.1, bf16[4096]{0:T(1024)(128)(2,1)} %gain_ref.1, ...), custom_call_target="tpu_custom_call" | custom-call | tf_op jit(solution)/shard_map/cross_attention_grads/pallas_call | solution.py:794
  72.6 2.2 %hand_on.1 = (bf16[256,512]{1,0:T(8,128)(2,1)}, bf16[32,4096]{1,0:T(8,128)(2,1)}, f32[256,512]{1,0:T(8,128)}, f32[256,512]{1,0:T(8,128)}) custom-call(bf16[256,512]{1,0:T(8,128)(2,1)} %get-tuple-element.8.a, bf16[32,4096]{1,0:T(8,128)(2,1)} %get-tuple-element.9.b, f32[256,512]{1,0:T(8,128)} %get-tuple-element.10.c, f32[256,512]{1,0:T(8,128)} %get-tuple-element.11.d), custom_call_target="tpu_custom_call" | custom-call | tf_op jit(solution)/shard_map/hand_on/pallas_call | solution.py:901
